TPU v7x, 256 devices: a whole 4x4x8 slice. The times are simulated.
256 devices in a mesh: row: 32 (over x, y, core), col: 8 (over z).
Axes of the slice: x: 4, y: 4, z: 8, core: 2. Of those that a mesh axis runs over, the one named last changes fastest.
Arguments:
- in_map: bfloat16 [512, 256, 256], P('row', 'col'), may hold values from -6 to 6
- tile_w: bfloat16 [3, 3, 256, 256], replicated, may hold values from -0.125 to 0.125
- head_w1: bfloat16 [3, 3, 256, 256], replicated, may hold values from -0.125 to 0.125
- head_w2: bfloat16 [3, 3, 256, 256], replicated, may hold values from -0.125 to 0.125
- box_row: int32 [512, 8], P('row', 'col'), may hold values from 0 to 2
- box_col: int32 [512, 8], P('row', 'col'), may hold values from 0 to 18
- box_target: int32 [512, 8], P('row', 'col'), may hold values from -1 to 31, as said below
- head_cot: bfloat16 [128, 8, 14, 14, 256], P('row', 'col'), may hold values from -6 to 6
Outputs:
- grad_map: bfloat16 [512, 256, 256], P('row', 'col')
- grad_w1: float32 [3, 3, 256, 256], replicated
- grad_w2: float32 [3, 3, 256, 256], replicated
Inputs may be any that keep to these rules, and one draw needn't show every extreme that they name: `box_target`: within each row r of tiles, every head slot d * 4 + h (d below 8, h below 4) is named by exactly one tile slot, and empty slots hold -1. A tile names at most 2 head slots of one device, so it holds at most 16 boxes; in every row of tiles one tile holds 16 boxes, 2 for each device of the row.
All inputs are finite; a program needn't handle non-finite values.
Results may differ from a plain program's by a relative error of at most 0.012.
Values may be sent and summed in bfloat16 or wider, within the bound.
A program may use at most 64 MiB of HBM per device.

v0:
```python
import math

import jax
import jax.numpy as jnp
from jax import lax
from jax.sharding import PartitionSpec as P

LAYOUT = ("NHWC", "HWIO", "NHWC")


def padded_2(shard, sides, width):
    for axis, dim in sides:
        size, length = (lax.axis_size(axis), shard.shape[dim])
        up = [(i, (i + 1) % size) for i in range(size - 1)]
        down = [(j, i) for i, j in up]
        last = lax.slice_in_dim(shard, length - width, length, axis=dim)
        leading = lax.slice_in_dim(shard, 0, width, axis=dim)
        before = lax.ppermute(last, axis, up)
        after = lax.ppermute(leading, axis, down)
        shard = jnp.concatenate([before, shard, after], axis=dim)
    return shard


def conv_pad(inputs, kernel, margin):
    return lax.conv_general_dilated(
        inputs,
        kernel,
        (1, 1),
        ((margin, margin), (margin, margin)),
        dimension_numbers=LAYOUT,
        preferred_element_type=jnp.float32,
    )


def flip_weights(kernel):
    return jnp.transpose(jnp.flip(kernel, (0, 1)), (0, 1, 3, 2))


def silu_slope(values):
    sigma = jax.nn.sigmoid(values)
    return sigma * (1.0 + values * (1.0 - sigma))


def weight_grad(inputs, deltas):
    channels = inputs.shape[-1]
    box_side = inputs.shape[1]
    padded = jnp.pad(inputs, ((0, 0), (1, 1), (1, 1), (0, 0)))
    flat_delta = deltas.reshape(-1, channels)
    blocks = []
    for shift_y in range(3):
        for shift_x in range(3):
            window = padded[
                :, shift_y : shift_y + box_side, shift_x : shift_x + box_side, :
            ].reshape(-1, channels)
            blocks.append(
                lax.dot_general(
                    window, flat_delta, (((0,), (0,)), ((), ())), preferred_element_type=jnp.float32
                )
            )
    return jnp.stack(blocks).reshape(3, 3, channels, channels)


def pick_rows(table, values):
    flat = values.reshape(values.shape[0], -1)
    return jnp.dot(table, flat, preferred_element_type=jnp.float32).astype(jnp.bfloat16)


def pick_back(table, values):
    return lax.dot_general(
        table, values, (((0,), (0,)), ((), ())), preferred_element_type=jnp.float32
    ).astype(jnp.bfloat16)


def body(in_map, tile_w, head_w1, head_w2, box_row, box_col, box_target, head_cot):
    tile_rows, tile_cols, channels = in_map.shape
    head_count = head_cot.shape[0]
    box_side = head_cot.shape[2]
    slot_count = box_target.shape[0]
    columns = lax.axis_size("col")
    capacity = slot_count // columns
    pair_count = columns * capacity
    padded = padded_2(in_map, (("row", 0), ("col", 1)), 1)
    preact = conv_pad(padded[None], tile_w, 0)[0]
    target = box_target[:, 0]
    occupied = target >= 0
    dest_col = jnp.where(occupied, target // head_count, 0)
    head_slot = jnp.where(occupied, target % head_count, 0)
    slot_ids = jnp.arange(slot_count, dtype=jnp.int32)
    same_dest = (dest_col[:, None] == dest_col[None, :]) & occupied[None, :]
    placing = jnp.sum(same_dest & (slot_ids[None, :] < slot_ids[:, None]), axis=1)
    pair_slot = dest_col * capacity + placing
    pair_ids = jnp.arange(pair_count, dtype=jnp.int32)
    send_map = ((pair_slot[None, :] == pair_ids[:, None]) & occupied[None, :]).astype(jnp.bfloat16)
    head_ids = jnp.arange(head_count, dtype=jnp.int32)
    head_hot = ((head_slot[:, None] == head_ids[None, :]) & occupied[:, None]).astype(jnp.bfloat16)
    pair_head = (
        jnp.dot(send_map, head_hot, preferred_element_type=jnp.float32)
        .astype(jnp.bfloat16)
        .reshape(columns, capacity, head_count)
    )
    top_row = box_row[:, 0]
    left_col = box_col[:, 0]
    zero_index = jnp.zeros((), jnp.int32)
    feature = jax.nn.silu(preact).astype(jnp.bfloat16)
    crops = jax.vmap(
        lambda y, x: lax.dynamic_slice(feature, (y, x, zero_index), (box_side, box_side, channels))
    )(top_row, left_col)
    outgoing = pick_rows(send_map, crops).reshape(columns, capacity, box_side, box_side, channels)
    arrived, arrived_head = (
        lax.all_to_all(outgoing, "col", split_axis=0, concat_axis=0, tiled=True),
        lax.all_to_all(pair_head, "col", split_axis=0, concat_axis=0, tiled=True),
    )
    arrived_head = arrived_head.reshape(pair_count, head_count)
    box_input = pick_back(arrived_head, arrived.reshape(pair_count, -1)).reshape(
        head_count, box_side, box_side, channels
    )
    factor = 1.0 / math.sqrt(lax.axis_size("row") * columns * head_count * box_side * box_side)
    cotangent = head_cot[:, 0]
    pre_one = conv_pad(box_input, head_w1, 1)
    hidden = jax.nn.silu(pre_one).astype(jnp.bfloat16)
    pre_two = conv_pad(hidden, head_w2, 1)
    delta_two = (cotangent.astype(jnp.float32) * silu_slope(pre_two)).astype(jnp.bfloat16)
    second_local = weight_grad(hidden, delta_two)
    delta_one = (conv_pad(delta_two, flip_weights(head_w2), 1) * silu_slope(pre_one)).astype(
        jnp.bfloat16
    )
    box_grads = conv_pad(delta_one, flip_weights(head_w1), 1).astype(jnp.bfloat16)
    sent_back = pick_rows(arrived_head, box_grads).reshape(
        columns, capacity, box_side, box_side, channels
    )
    returned = lax.all_to_all(sent_back, "col", split_axis=0, concat_axis=0, tiled=True)
    slot_grads = pick_back(send_map, returned.reshape(pair_count, -1)).reshape(
        slot_count, box_side, box_side, channels
    )
    first_local = weight_grad(box_input, delta_one)
    first_sum, second_sum = lax.psum((first_local, second_local), ("row", "col"))

    def add_box(slot, running):
        current = lax.dynamic_slice(
            running, (top_row[slot], left_col[slot], zero_index), (box_side, box_side, channels)
        )
        return lax.dynamic_update_slice(
            running,
            current + slot_grads[slot].astype(jnp.float32),
            (top_row[slot], left_col[slot], zero_index),
        )

    box_total = lax.fori_loop(
        0, slot_count, add_box, jnp.zeros((tile_rows, tile_cols, channels), jnp.float32)
    )
    delta_map = (box_total * silu_slope(preact)).astype(jnp.bfloat16)
    delta_rim = padded_2(delta_map, (("row", 0), ("col", 1)), 1)
    grad_map = conv_pad(delta_rim[None], flip_weights(tile_w), 0)[0].astype(jnp.bfloat16)
    return (grad_map, first_sum * factor, second_sum * factor)


def solution(mesh):
    in_specs = (
        P("row", "col", None),
        P(),
        P(),
        P(),
        P("row", "col"),
        P("row", "col"),
        P("row", "col"),
        P("row", "col", None, None, None),
    )
    out_specs = (P("row", "col", None), P(), P())
    return jax.shard_map(body, mesh=mesh, in_specs=in_specs, out_specs=out_specs, check_vma=False)
```

profile of v0, /device:TPU:1, one launch (start us, length us, event | category | flops | bytes accessed | tf_op | source)
XLA Modules:
  0.0 487.0 jit_solution(9538092367469643481)
XLA Ops:
  8.0 5.1 %collective-permute-start.1 = (bf16[1,32,256]{2,1,0:T(8,128)(2,1)S(1)}, bf16[1,32,256]{2,1,0:T(8,128)(2,1)S(1)}, u32[]{:S(2)}, u32[]{:S(2)}) collective-permute-start(bf16[1,32,256]{2,1,0:T(8,128)(2,1)S(1)} %get-tuple-element.161), channel_id=1, source_target_pairs={{8,0},{16,8},{24,16},{32,24},{40,32},{48,40},{56,48},{64,56},{72,6... | collective-permute-start | bytes 49160 | tf_op jit(solution)/shard_map/ppermute | solution.py:19
  13.2 1.9 collective-permute-start
  19.7 3.1 collective-permute-start.2
  22.8 1.3 collective-permute-start.3
  24.2 3.6 collective-permute-done.3
  30.4 41.9 %while.15 = (s32[]{:T(128)}, bf16[16,32,256]{2,0,1:T(8,128)(2,1)S(1)}, s32[16,3]{0,1:T(4,128)S(1)}, bf16[16,14,14,256]{3,2,1,0:T(8,128)(2,1)}, s32[]{:T(128)}) while((s32[]{:T(128)}, bf16[16,32,256]{2,0,1:T(8,128)(2,1)S(1)}, s32[16,3]{0,1:T(4,128)S(1)}, bf16[16,14,14,256]{3,2,1,0:T(8,128)(2,1)}, s32[]{:T(128)}) %tuple.61), condition=%wide.while_cond, body=%wide.while_body.sunk | while | flops 2 | bytes 415869 | solution.py:106
  31.0 1.3 constant_dynamic-slice_fusion.8
  33.6 1.3 constant_dynamic-slice_fusion.8
  36.2 1.3 constant_dynamic-slice_fusion.8
  38.8 1.3 constant_dynamic-slice_fusion.8
  41.5 1.3 constant_dynamic-slice_fusion.8
  44.1 1.3 constant_dynamic-slice_fusion.8
  46.7 1.3 constant_dynamic-slice_fusion.8
  49.3 1.3 constant_dynamic-slice_fusion.8
  51.9 1.3 constant_dynamic-slice_fusion.8
  54.6 1.3 constant_dynamic-slice_fusion.8
  57.2 1.3 constant_dynamic-slice_fusion.8
  59.8 1.3 constant_dynamic-slice_fusion.8
  62.4 1.3 constant_dynamic-slice_fusion.8
  65.0 1.3 constant_dynamic-slice_fusion.8
  67.6 1.3 constant_dynamic-slice_fusion.8
  70.3 1.3 constant_dynamic-slice_fusion.8
  72.3 2.4 reshape.125
  74.7 1.7 convolution_convert_fusion.1
  76.4 2.6 reshape.126
  79.0 3.6 copy.100
  82.7 8.2 %all-to-all-start.1 = ((bf16[8,2,14,14,256]{4,1,3,2,0:T(2,128)(2,1)}), bf16[8,2,14,14,256]{4,1,3,2,0:T(2,128)(2,1)}, u32[]{:S(2)}, u32[]{:S(2)}) async-start(bf16[8,2,14,14,256]{4,1,3,2,0:T(2,128)(2,1)} %copy.100), calls=%async_computation.1 | async-start | bytes 3211264 | tf_op jit(solution)/shard_map/all_to_all | solution.py:110
  91.8 38.0 %all-to-all-done.1 = bf16[8,2,14,14,256]{4,1,3,2,0:T(2,128)(2,1)} async-done(((bf16[8,2,14,14,256]{4,1,3,2,0:T(2,128)(2,1)}), bf16[8,2,14,14,256]{4,1,3,2,0:T(2,128)(2,1)}, u32[]{:S(2)}, u32[]{:S(2)}) %all-to-all-start.1) | async-done | bytes 1605664 | tf_op jit(solution)/shard_map/all_to_all | solution.py:110
  129.9 3.6 all-to-all-start
  133.4 1.7 copy.101
  135.2 2.1 reshape.127
  137.3 2.6 all-to-all-done
  139.9 1.8 convolution_convert_fusion.3
  144.7 1.2 convolution_select_fusion.1
  145.9 1.1 select_bitcast_fusion.1
  147.1 1.3 add_multiply_fusion
  149.8 1.2 fusion.51
  152.9 1.3 fusion.8
  155.1 1.1 fusion.27
  158.6 1.3 convolution_convert_fusion.4
  161.4 1.7 reshape.130
  163.2 3.7 copy.109
  166.8 4.2 all-to-all-start.2
  171.0 1.1 fusion.26
  172.1 1.1 fusion.25
  174.3 1.1 fusion.23
  176.4 1.1 fusion.21
  178.5 1.1 fusion.19
  181.7 1.1 fusion.16
  185.9 1.1 fusion.12
  187.0 1.0 fusion.11
  188.0 1.1 fusion.10
  189.1 22.2 %all-to-all-done.2 = bf16[8,2,14,14,256]{4,1,3,2,0:T(2,128)(2,1)S(1)} async-done(((bf16[8,2,14,14,256]{4,1,3,2,0:T(2,128)(2,1)}), bf16[8,2,14,14,256]{4,1,3,2,0:T(2,128)(2,1)S(1)}, u32[]{:S(2)}, u32[]{:S(2)}) %all-to-all-start.2) | async-done | bytes 1605664 | tf_op jit(solution)/shard_map/all_to_all | solution.py:131
  211.6 1.2 reshape.131
  213.5 1.5 reshape.132
  215.2 90.9 %while.14 = (s32[]{:T(128)}, f32[16,32,256]{2,0,1:T(8,128)S(1)}, s32[16]{0:T(128)S(1)}, s32[16]{0:T(128)S(1)}, bf16[16,14,14,256]{3,2,1,0:T(8,128)(2,1)S(1)}, /*index=5*/s32[]{:T(128)}, s32[]{:T(128)}, s32[]{:T(128)}, s32[]{:T(128)}) while((s32[]{:T(128)}, f32[16,32,256]{2,0,1:T(8,128)S(1)}, s32[16]{0:T(128)S(1)}, s32[16]{0:T(128)S(1)}, ...), condition=%wide.region_2.3_spmd, body=%wide.region_1.2_spmd.sunk | while | flops 100360 | bytes 1706193 | solution.py:148
  306.3 4.0 collective-permute-start.4
  310.4 1.9 collective-permute-start.5
  312.3 153.4 %all-reduce.5.cloned.1.call-done = (f32[3,3,256,256]{3,2,1,0:T(8,128)}, f32[3,3,256,256]{3,2,1,0:T(8,128)}) async-done(((f32[3,3,256,256]{3,2,1,0:T(8,128)}, f32[3,3,256,256]{3,2,1,0:T(8,128)}), (f32[3,3,256,256]{3,2,1,0:T(8,128)}, f32[3,3,256,256]{3,2,1,0:T(8,128)})) %all-reduce.5.cloned.1.call-update) | async-done | bytes 4718608 | tf_op jit(solution)/shard_map/psum | solution.py:136
  465.7 3.4 broadcast_multiply_fusion.1
  469.1 3.3 collective-permute-start.6
  472.4 1.3 collective-permute-start.7
  473.7 1.6 broadcast_multiply_fusion
  475.3 2.6 collective-permute-done.7
  (279 shorter events, 80.6 us)
Async XLA Ops:
  7.2 139.9 %copy-start = (bf16[3,3,256,256]{3,2,1,0:T(8,128)(2,1)S(1)}, bf16[3,3,256,256]{3,2,1,0:T(8,128)(2,1)}, u32[]{:S(2)}) copy-start(bf16[3,3,256,256]{3,2,1,0:T(8,128)(2,1)} %param.13) | copy-start | bytes 3538948
  8.0 11.6 %collective-permute-start.1 = (bf16[1,32,256]{2,1,0:T(8,128)(2,1)S(1)}, bf16[1,32,256]{2,1,0:T(8,128)(2,1)S(1)}, u32[]{:S(2)}, u32[]{:S(2)}) collective-permute-start(bf16[1,32,256]{2,1,0:T(8,128)(2,1)S(1)} %get-tuple-element.161), channel_id=1, source_target_pairs={{8,0},{16,8},{24,16},{32,24},{40,32},{48,40},{56,48},{64,56},{72,6... | collective-permute-start | bytes 49160 | tf_op jit(solution)/shard_map/ppermute | solution.py:19
  13.2 5.4 %collective-permute-start = (bf16[1,32,256]{2,1,0:T(8,128)(2,1)S(1)}, bf16[1,32,256]{2,1,0:T(8,128)(2,1)S(1)}, u32[]{:S(2)}, u32[]{:S(2)}) collective-permute-start(bf16[1,32,256]{2,1,0:T(8,128)(2,1)S(1)} %get-tuple-element.162), channel_id=1, source_target_pairs={{0,8},{8,16},{16,24},{24,32},{32,40},{40,48},{48,56},{56,64},{64,7... | collective-permute-start | bytes 49160 | tf_op jit(solution)/shard_map/ppermute | solution.py:18
  19.6 8.6 %copy-start.22 = (bf16[3,3,256,256]{3,2,1,0:T(8,128)(2,1)S(1)}, bf16[3,3,256,256]{3,2,1,0:T(8,128)(2,1)}, u32[]{:S(2)}) copy-start(bf16[3,3,256,256]{3,2,1,0:T(8,128)(2,1)} %param.11) | copy-start | bytes 3538948
  19.6 8.6 %copy-start.25 = (pred[8,5]{0,1:T(8,128)(4,1)S(1)}, pred[8,5]{0,1:T(8,128)(4,1)}, u32[]{:S(2)}) copy-start(pred[8,5]{0,1:T(8,128)(4,1)} %constant.124) | copy-start | bytes 124
  19.7 4.5 collective-permute-start.2
  22.8 4.9 %collective-permute-start.3 = (bf16[18,1,256]{2,1,0:T(2,128)(2,1)S(1)}, bf16[18,1,256]{2,1,0:T(2,128)(2,1)S(1)}, u32[]{:S(2)}, u32[]{:S(2)}) collective-permute-start(bf16[18,1,256]{2,1,0:T(2,128)(2,1)S(1)} %get-tuple-element.158), channel_id=1, source_target_pairs={{1,0},{2,1},{3,2},{4,3},{5,4},{6,5},{7,6},{9,8},{10,9},{11,10},{12... | collective-permute-start | bytes 27656 | tf_op jit(solution)/shard_map/ppermute | solution.py:19
  29.4 0.8 copy-start.2
  82.7 8.2 %copy-start.24 = (s32[16,1]{0,1:T(1,128)S(1)}, s32[16,1]{0,1:T(1,128)}, u32[]{:S(2)}) copy-start(s32[16,1]{0,1:T(1,128)} %param.16) | copy-start | bytes 196
  82.7 47.2 %all-to-all-start.1 = ((bf16[8,2,14,14,256]{4,1,3,2,0:T(2,128)(2,1)}), bf16[8,2,14,14,256]{4,1,3,2,0:T(2,128)(2,1)}, u32[]{:S(2)}, u32[]{:S(2)}) async-start(bf16[8,2,14,14,256]{4,1,3,2,0:T(2,128)(2,1)} %copy.100), calls=%async_computation.1 | async-start | bytes 3211264 | tf_op jit(solution)/shard_map/all_to_all | solution.py:110
  129.9 10.0 %all-to-all-start = ((bf16[8,2,4]{2,1,0:T(2,128)(2,1)}), bf16[8,2,4]{2,1,0:T(2,128)(2,1)S(1)}, u32[]{:S(2)}, u32[]{:S(2)}) async-start(bf16[8,2,4]{2,1,0:T(2,128)(2,1)} %bitcast.9), calls=%async_computation | async-start | bytes 8192 | tf_op jit(solution)/shard_map/all_to_all | solution.py:111
  143.0 12.1 %copy-start.8 = (bf16[4,14,14,256]{3,2,1,0:T(8,128)(2,1)}, bf16[4,14,14,256]{3,2,1,0:T(8,128)(2,1)S(1)}, u32[]{:S(2)}) copy-start(bf16[4,14,14,256]{3,2,1,0:T(8,128)(2,1)S(1)} %reshape.128) | copy-start | bytes 1204228
  143.0 0.7 copy-start.17
  143.4 1.3 copy-start.20
  145.9 1.2 copy-start.13
  150.9 0.8 copy-start.10
  151.7 1.2 copy-start.14
  155.0 1.1 copy-start.6
  155.1 1.1 copy-start.12
  156.1 2.4 copy-start.21
  166.8 4.2 copy-start.7
  166.8 4.2 copy-start.9
  166.8 44.5 %all-to-all-start.2 = ((bf16[8,2,14,14,256]{4,1,3,2,0:T(2,128)(2,1)}), bf16[8,2,14,14,256]{4,1,3,2,0:T(2,128)(2,1)S(1)}, u32[]{:S(2)}, u32[]{:S(2)}) async-start(bf16[8,2,14,14,256]{4,1,3,2,0:T(2,128)(2,1)} %copy.109), calls=%async_computation.2 | async-start | bytes 3211264 | tf_op jit(solution)/shard_map/all_to_all | solution.py:131
  171.0 294.7 %all-reduce.5.cloned.1.call-start = ((), (), s32[]{:S(2)}) async-start(), calls=%async_computation.3 | async-start | bytes 9437184 | tf_op jit(solution)/shard_map/psum | solution.py:136
  173.1 1.0 copy-start.15
  173.2 1.1 copy-start.16
  178.5 1.1 copy-start.5
  178.5 1.2 copy-start.11
  213.5 1.6 copy-start.18
  213.5 1.6 copy-start.19
  215.1 90.9 %copy-start.3 = (f32[16,8,5,256]{3,0,2,1:T(8,128)S(1)}, f32[16,8,5,256]{3,0,2,1:T(8,128)}, u32[]{:S(2)}) copy-start(f32[16,8,5,256]{3,0,2,1:T(8,128)} %copy-done.2) | copy-start | bytes 1966084
  306.3 162.8 %collective-permute-start.4 = (bf16[1,32,256]{2,0,1:T(2,128)(2,1)S(1)}, bf16[1,32,256]{2,0,1:T(2,128)(2,1)S(1)}, u32[]{:S(2)}, u32[]{:S(2)}) collective-permute-start(bf16[1,32,256]{2,0,1:T(2,128)(2,1)S(1)} %get-tuple-element.159), channel_id=1, source_target_pairs={{0,8},{8,16},{16,24},{24,32},{32,40},{40,48},{48,56},{56,64},{64,7... | collective-permute-start | bytes 49160 | tf_op jit(solution)/shard_map/ppermute | solution.py:18
  310.4 158.7 %collective-permute-start.5 = (bf16[1,32,256]{2,0,1:T(2,128)(2,1)S(1)}, bf16[1,32,256]{2,0,1:T(2,128)(2,1)S(1)}, u32[]{:S(2)}, u32[]{:S(2)}) collective-permute-start(bf16[1,32,256]{2,0,1:T(2,128)(2,1)S(1)} %get-tuple-element.160), channel_id=1, source_target_pairs={{8,0},{16,8},{24,16},{32,24},{40,32},{48,40},{56,48},{64,56},{72,6... | collective-permute-start | bytes 49160 | tf_op jit(solution)/shard_map/ppermute | solution.py:19
  465.7 8.1 %copy-start.4 = (f32[3,3,256,256]{3,2,1,0:T(8,128)S(1)}, f32[3,3,256,256]{3,2,1,0:T(8,128)}, u32[]{:S(2)}) copy-start(f32[3,3,256,256]{3,2,1,0:T(8,128)} %get-tuple-element.146) | copy-start | bytes 7077892
  469.1 6.2 %collective-permute-start.6 = (bf16[18,1,256]{2,0,1:T(8,128)(2,1)S(1)}, bf16[18,1,256]{2,0,1:T(8,128)(2,1)S(1)}, u32[]{:S(2)}, u32[]{:S(2)}) collective-permute-start(bf16[18,1,256]{2,0,1:T(8,128)(2,1)S(1)} %get-tuple-element.155), channel_id=1, source_target_pairs={{0,1},{1,2},{2,3},{3,4},{4,5},{5,6},{6,7},{8,9},{9,10},{10,11},{11... | collective-permute-start | bytes 27656 | tf_op jit(solution)/shard_map/ppermute | solution.py:18
  472.4 5.5 %collective-permute-start.7 = (bf16[18,1,256]{2,0,1:T(8,128)(2,1)S(1)}, bf16[18,1,256]{2,0,1:T(8,128)(2,1)S(1)}, u32[]{:S(2)}, u32[]{:S(2)}) collective-permute-start(bf16[18,1,256]{2,0,1:T(8,128)(2,1)S(1)} %get-tuple-element.156), channel_id=1, source_target_pairs={{1,0},{2,1},{3,2},{4,3},{5,4},{6,5},{7,6},{9,8},{10,9},{11,10},{12... | collective-permute-start | bytes 27656 | tf_op jit(solution)/shard_map/ppermute | solution.py:19
  475.3 3.0 copy-start.23
  478.3 1.9 copy-start.1
Sparse Core Ops, SparseCore 0:
  189.2 276.4 all-reduce.4
where the time goes:
time: 491 us; the launch traced here: 487 us
  waiting for transfers between devices  222 us (45%)
  local copies, waits for them, and re-layouts  104 us (21%)
  loops' own time  63.1 us (13%)
  starting transfers between devices  38 us (8%)
  matrix products  30.9 us (6%)
  between operations  14.8 us (3%)
  other arithmetic  13.8 us (3%)
    psum x1, waiting for transfers between devices, body(): lax.psum((first_local, second_local), ('row', 'col'))  153 us
    another operation x1, loops' own time, body(): lax.fori_loop(0, slot_count, add_box, jnp.zeros((tile_rows, tile_cols, ch...  62.9 us
    gather x64, local copies, waits for them, and re-layouts  41.8 us
    all_to_all x1, waiting for transfers between devices, body(): lax.all_to_all(outgoing, 'col', split_axis=0, concat_axis=0, tiled=True)  38 us
    all_to_all x1, waiting for transfers between devices, body(): lax.all_to_all(sent_back, 'col', split_axis=0, concat_axis=0, tiled=True)  22.2 us
    dot_general x18, matrix products, weight_grad(): lax.dot_general(window, flat_delta, (((0,), (0,)), ((), ())), preferred_e...  18.9 us
    ppermute x4, starting transfers between devices, padded_2(): before = lax.ppermute(last, axis, up)  12.4 us
  transfers between devices with their start and end apart: 12, of which 6 were waited for; matrix products, arithmetic and copies ran while one was open for 13% of the time, Pallas kernels for 0%

commit v1 on v0

v1 whole, which is shorter than its diff:
```python
import math

import jax
import jax.numpy as jnp
from jax import lax
from jax.experimental import pallas as pl
from jax.experimental.pallas import tpu as pltpu
from jax.sharding import PartitionSpec as P

MESH = pl.DeviceIdType.MESH
BF = jnp.bfloat16
F32 = jnp.float32
NZ = 8
NX = 4
NY = 4
NROW = 32
PX = 512
HALF = 256
POS = 256
CH = 256
K_HALO = 0
K_TAB = 16
K_AG = 23
K_RS = 37
K_AR = 51
AR_N = 28
N_SEM = K_AR + 2 * AR_N


def silu_slope(values):
    sigma = jax.nn.sigmoid(values)
    return sigma * (1.0 + values * (1.0 - sigma))


def mm(a, b):
    return jnp.dot(a, b, preferred_element_type=F32)


def kernel(
    in_ref, tw_ref, w1_ref, w2_ref, brow_ref, bcol_ref, btgt_ref, cot_ref,
    gmap_ref, gsum_ref,
    xf, xp, x3m, slope_map, scol, hrow, hcol, hl, hr,
    tab, gcol, grow, feats, acc, xc3, xh3, d23, d13, slope1, cotp, xt,
    twt, w1t, w2t, bg, rs_s, rs_r, dm,
    own, snd, rc, s1, r1, t2, s2, r2, t3, s3, r3, zb,
    ssem, rsem,
):
    row = lax.axis_index("row")
    me = lax.axis_index("col")
    px = row // 8
    py = lax.rem(row // 2, NY)
    core = lax.rem(row, 2)

    def at_x(d):
        return (lax.rem(px + d, NX) * 8 + py * 2 + core, me)

    def at_y(d):
        return (px * 8 + lax.rem(py + d, NY) * 2 + core, me)

    def at_z(d):
        return (row, lax.rem(me + d + NZ, NZ))

    sibling = (row + 1 - 2 * core, me)

    def near(dr, dc):
        return (lax.rem(row + dr + NROW, NROW), lax.rem(me + dc + NZ, NZ))

    live = {}

    def send(src, dst, k, dev):
        copy = pltpu.make_async_remote_copy(
            src_ref=src, dst_ref=dst, send_sem=ssem.at[k], recv_sem=rsem.at[k],
            device_id=dev, device_id_type=MESH,
        )
        copy.start()
        live[k] = copy

    def got(k):
        live[k].wait_recv()

    halo_dirs = [(1, 0), (-1, 0), (1, 1), (0, 1), (-1, 1), (1, -1), (0, -1), (-1, -1)]

    barrier = pltpu.get_barrier_semaphore()
    partners = [near(*d) for d in halo_dirs]
    partners += [at_z(d) for d in range(2, 7)]
    partners += [at_x(d) for d in range(1, 4)] + [at_y(d) for d in range(1, 4)] + [sibling]
    for dev in partners:
        pl.semaphore_signal(barrier, inc=1, device_id=dev, device_id_type=MESH)

    xf[...] = in_ref[...].astype(F32)
    scol[0, 0] = xf[:, 31, :].astype(BF)
    scol[0, 1] = xf[:, 0, :].astype(BF)
    code = btgt_ref[...] * 128 + brow_ref[...] * 32 + bcol_ref[...]
    tab[0] = jnp.broadcast_to(code, (16, 128))
    for buf in (xc3, xh3, d23, d13):
        buf[...] = jnp.zeros_like(buf)
    acc[...] = jnp.zeros_like(acc)
    xp[pl.ds(32, PX), :] = in_ref[...].reshape(PX, CH)

    pl.semaphore_wait(barrier, len(partners))

    def halo_send(t, img):
        base = K_HALO + 8 * t
        for i, d in enumerate(halo_dirs):
            if i < 2:
                send(img.at[15 if i == 0 else 0], hrow.at[t, i], base + i, near(*d))
            else:
                send(scol.at[t, 0 if i < 5 else 1], hcol.at[t, i - 2], base + i, near(*d))

    def halo_recv(t):
        base = K_HALO + 8 * t
        for i in range(8):
            got(base + i)
        above, below = row > 0, row < NROW - 1
        left, right = me > 0, me < NZ - 1

        def part(ok, v):
            return jnp.where(ok, v, jnp.zeros_like(v))

        xp[pl.ds(0, 32), :] = part(above, hrow[t, 0])
        xp[pl.ds(544, 32), :] = part(below, hrow[t, 1])
        for side, ok, dst in ((0, left, hl), (3, right, hr)):
            dst[0:1, :] = part(ok & above, hcol[t, side].astype(F32)[15:16, :])
            dst[1:17, :] = part(ok, hcol[t, side + 1].astype(F32))
            dst[17:18, :] = part(ok & below, hcol[t, side + 2].astype(F32)[0:1, :])

        lanes = lax.broadcasted_iota(jnp.int32, (32, CH), 0)

        def one(r, carry):
            at = pl.multiple_of(r * 32, 32)
            mid = xp[pl.ds(at, 32), :]
            c = mid.astype(F32)
            lf = jnp.where(lanes == 0, hl[pl.ds(r, 1), :], pltpu.roll(c, 1, 0))
            rt = jnp.where(lanes == 31, hr[pl.ds(r, 1), :], pltpu.roll(c, 31, 0))
            x3m[pl.ds(at, 32), 0:CH] = lf.astype(BF)
            x3m[pl.ds(at, 32), CH:2 * CH] = mid
            x3m[pl.ds(at, 32), 2 * CH:3 * CH] = rt.astype(BF)
            return carry

        lax.fori_loop(0, 18, one, 0)

    def conv_map(w, j):
        total = mm(x3m[pl.ds(j * HALF, HALF), :], w[0])
        total += mm(x3m[pl.ds(j * HALF + 32, HALF), :], w[1])
        total += mm(x3m[pl.ds(j * HALF + 64, HALF), :], w[2])
        return total

    def turn(src, dst):
        def one(a, carry):
            for b in range(3):
                dst[a, b * CH:(b + 1) * CH, :] = src[2 - a, (2 - b) * CH:(3 - b) * CH, :].T
            return carry

        lax.fori_loop(0, 3, one, 0)

    halo_send(0, in_ref)
    for d in range(1, NZ):
        send(tab.at[0], tab.at[d], K_TAB + d - 1, at_z(d))
    turn(w2_ref, w2t)
    halo_recv(0)

    def ag_key(right, s, j):
        return K_AG + (0 if right else 7) + (s * 2 + j if s < 3 else 6)

    def ag_send(right, s, j):
        src = feats.at[s if right else (NZ - s) % NZ, pl.ds(j * HALF, HALF), :]
        dst = feats.at[s + 1 if right else NZ - 1 - s, pl.ds(j * HALF, HALF), :]
        send(src, dst, ag_key(right, s, j), at_z(1 if right else -1))

    for j in range(2):
        pre = conv_map(tw_ref, j)
        feats[0, pl.ds(j * HALF, HALF), :] = (pre * jax.nn.sigmoid(pre)).astype(BF)
        slope_map[pl.ds(j * HALF, HALF), :] = silu_slope(pre)
        ag_send(True, 0, j)
        ag_send(False, 0, j)

    for d in range(1, NZ):
        got(K_TAB + d - 1)
    for h in range(4):
        base = jnp.zeros((1, 128), jnp.int32)
        for s in range(NZ):
            tile = lax.rem(me - s + NZ, NZ)
            word = tab[s]
            hit = (word >> 7) == me * 4 + h
            value = (word & 127) + tile * PX
            base += jnp.sum(jnp.where(hit, value, 0), axis=0, keepdims=True)
        p = lax.broadcasted_iota(jnp.int32, (POS, 128), 0)
        i, j = p >> 4, p & 15
        ok = (i >= 1) & (i <= 14) & (j < 14)
        gcol[h] = jnp.where(ok, base + (i - 1) * 32 + j, -1)
        p = lax.broadcasted_iota(jnp.int32, (1, POS), 1)
        i, j = p >> 4, p & 15
        ok = (i >= 1) & (i <= 14) & (j < 14)
        both = jnp.concatenate([base, base], axis=1)
        grow[0:1, h * POS:(h + 1) * POS] = jnp.where(ok, both + (i - 1) * 32 + j, -1)

    def take(s, j):
        tile = lax.rem(me - s + NZ, NZ)
        first = tile * PX + j * HALF

        def one(h, carry):
            q = lax.broadcasted_iota(jnp.int32, (POS, 128), 1) + first
            g = gcol[h]
            hot = jnp.concatenate(
                [jnp.where(g == q, 1.0, 0.0), jnp.where(g == q + 128, 1.0, 0.0)], axis=1
            ).astype(BF)
            acc[h] += mm(hot, feats[s, pl.ds(j * HALF, HALF), :])
            return carry

        lax.fori_loop(0, 4, one, 0)

    take(0, 0)
    take(0, 1)
    for s in range(1, 4):
        for j in range(2):
            got(ag_key(True, s - 1, j))
            if s < 3 or j == 0:
                ag_send(True, s, j)
            got(ag_key(False, s - 1, j))
            if s < 3 or j == 1:
                ag_send(False, s, j)
            take(s, j)
            take(NZ - s, j)
            if s == 1 and j == 0:
                turn(w1_ref, w1t)
            if s == 1 and j == 1:
                turn(tw_ref, twt)
    got(ag_key(True, 3, 0))
    take(4, 0)
    got(ag_key(False, 3, 1))
    take(4, 1)

    inside = (lax.broadcasted_iota(jnp.int32, (224, CH), 0) & 15) < 14

    def put(buf, h, value):
        at = pl.multiple_of(h * POS + 32, 16)
        mid = value.astype(BF)
        full = mid.astype(F32)
        buf[pl.ds(at, 224), 0:CH] = pltpu.roll(full, 1, 0).astype(BF)
        buf[pl.ds(at, 224), CH:2 * CH] = mid
        buf[pl.ds(at, 224), 2 * CH:3 * CH] = pltpu.roll(full, 223, 0).astype(BF)

    def conv_box(buf, w, h):
        at = pl.multiple_of(h * POS + 16, 16)
        total = mm(buf[pl.ds(at, 224), :], w[0])
        total += mm(buf[pl.ds(at + 16, 224), :], w[1])
        total += mm(buf[pl.ds(at + 32, 224), :], w[2])
        return total

    def cut(v):
        return jnp.where(inside, v, 0.0)

    def chain(h, carry):
        put(xc3, h, acc[h, 16:240, :])
        pre_one = conv_box(xc3, w1_ref, h)
        put(xh3, h, cut(pre_one * jax.nn.sigmoid(pre_one)))
        slope1[h] = silu_slope(pre_one)
        pre_two = conv_box(xh3, w2_ref, h)
        cotp[:, 0:14, :] = cot_ref[h, 0].astype(F32)
        cotp[:, 14:16, :] = jnp.zeros((14, 2, CH), F32)
        put(d23, h, cut(cotp[...].reshape(224, CH) * silu_slope(pre_two)))
        put(d13, h, cut(conv_box(d23, w2t, h) * slope1[h]))
        at = pl.multiple_of(h * POS, 16)
        bg[pl.ds(at, 16), :] = jnp.zeros((16, CH), BF)
        bg[pl.ds(at + 240, 16), :] = jnp.zeros((16, CH), BF)
        bg[pl.ds(at + 16, 224), :] = conv_box(d13, w1t, h).astype(BF)
        return carry

    lax.fori_loop(0, 4, chain, 0)

    def term(d, j):
        tile = lax.rem(me + d + NZ, NZ)
        q = lax.broadcasted_iota(jnp.int32, (HALF, 4 * POS), 0) + (tile * PX + j * HALF)
        hot = jnp.where(q == grow[0:1, :], 1.0, 0.0).astype(BF)
        return mm(hot, bg[...])

    def rs_item(right, k):
        if k == 0:
            d, j = 4, 0
        else:
            d = 3 - (k - 1) // 2
            j = 1 if k % 2 == 1 else 0
        return d, (j if right else 1 - j)

    def rs_key(right, k):
        return K_RS + (0 if right else 7) + k

    def rs_step(k):
        for right in (True, False):
            d, j = rs_item(right, k)
            side = 0 if right else 1
            value = term(d if right else -d, j)
            if k >= 2:
                got(rs_key(right, k - 2))
                value += rs_r[side, k - 2].astype(F32)
            rs_s[side, k] = value.astype(BF)
            send(rs_s.at[side, k], rs_r.at[side, k], rs_key(right, k), at_z(1 if right else -1))

    def wgrad(g, buf, dbuf):
        for h in range(4):
            xt[:, h * POS:(h + 1) * POS] = buf[16 + h * POS:16 + (h + 1) * POS, CH:2 * CH].T

        def one(a, carry):
            at = pl.multiple_of(32 - a * 16, 16)
            for b in range(3):
                value = mm(xt[...], dbuf[pl.ds(at, 4 * POS), (2 - b) * CH:(3 - b) * CH])
                low, high = value[:, 0:128], value[:, 128:256]
                own[g, a * 3 + b] = jnp.where(core == 0, low, high)
                snd[g, a * 3 + b] = jnp.where(core == 0, high, low).astype(BF)
            return carry

        lax.fori_loop(0, 3, one, 0)
        send(snd.at[g], rc.at[g], K_AR + g * AR_N, sibling)

    def axes(g):
        if g == 0:
            return at_x, px, NX, at_y, py, NY
        return at_y, py, NY, at_x, px, NX

    def ar1(g):
        k = K_AR + g * AR_N
        at1, p1, n1 = axes(g)[:3]
        got(k)

        def one(t, carry):
            v = own[g, t] + rc[g, t].astype(F32)
            own[g, t] = v
            s1[g, t] = v.astype(BF)
            return carry

        lax.fori_loop(0, 9, one, 0)
        for d in range(1, 4):
            q = lax.rem(p1 + d, n1)
            send(s1.at[g, :, pl.ds(q * 64, 64), :], r1.at[g, d - 1], k + d, at1(d))

    def ar2(g):
        k = K_AR + g * AR_N
        at1, p1, n1, at2, p2, n2 = axes(g)
        for d in range(1, 4):
            got(k + d)

        def one(t, carry):
            v = own[g, t, pl.ds(p1 * 64, 64), :]
            for d in range(3):
                v += r1[g, d, t].astype(F32)
            t2[g, t] = v
            s2[g, t] = v.astype(BF)
            return carry

        lax.fori_loop(0, 9, one, 0)
        for d in range(1, 4):
            q = lax.rem(p2 + d, n2)
            send(s2.at[g, :, pl.ds(q * 16, 16), :], r2.at[g, d - 1], k + 3 + d, at2(d))

    def ar3(g):
        k = K_AR + g * AR_N
        p2 = axes(g)[4]
        for d in range(1, 4):
            got(k + 3 + d)
        v = t2[g, :, pl.ds(p2 * 16, 16), :]
        for d in range(3):
            v += r2[g, d].astype(F32)
        t3[g, 0:9] = v
        t3[g, 9:16] = jnp.zeros((7, 16, 128), F32)
        s3[g, 0:9] = v.astype(BF)
        s3[g, 9:16] = jnp.zeros((7, 16, 128), BF)
        for d in range(1, NZ):
            q = lax.rem(me + d, NZ)
            send(s3.at[g, pl.ds(q * 2, 2)], r3.at[g, d - 1], k + 6 + d, at_z(d))

    def ar4(g):
        k = K_AR + g * AR_N
        for d in range(1, NZ):
            got(k + 6 + d)
        v = t3[g, pl.ds(me * 2, 2)]
        for d in range(NZ - 1):
            v += r3[g, d].astype(F32)
        zb[g, pl.ds(me * 2, 2)] = v.astype(BF)
        for d in range(1, NZ):
            part = zb.at[g, pl.ds(me * 2, 2)]
            send(part, part, k + 13 + d, at_z(d))

    def ar5(g):
        k = K_AR + g * AR_N
        at1, p1, n1, at2, p2, n2 = axes(g)
        for d in range(1, NZ):
            got(k + 13 + d)
        at = pl.multiple_of(p1 * 64 + p2 * 16, 16)
        gsum_ref[g, core, :, pl.ds(at, 16), :] = zb[g, 0:9]
        part = gsum_ref.at[g, core, :, pl.ds(at, 16), :]
        for d in range(1, 4):
            send(part, part, k + 20 + d, at2(d))

    def ar6(g):
        k = K_AR + g * AR_N
        at1, p1, n1 = axes(g)[:3]
        for d in range(1, 4):
            got(k + 20 + d)
        part = gsum_ref.at[g, core, :, pl.ds(p1 * 64, 64), :]
        for d in range(1, 4):
            send(part, part, k + 23 + d, at1(d))

    def ar7(g):
        k = K_AR + g * AR_N
        for d in range(1, 4):
            got(k + 23 + d)
        part = gsum_ref.at[g, core]
        send(part, part, k + 27, sibling)

    rs_step(0)
    rs_step(1)
    wgrad(1, xh3, d23)
    rs_step(2)
    wgrad(0, xc3, d13)
    rs_step(3)
    ar1(1)
    ar1(0)
    rs_step(4)
    rs_step(5)
    ar2(1)
    ar2(0)
    rs_step(6)
    ar3(1)
    ar3(0)

    for j in range(2):
        total = term(0, j)
        for right in (True, False):
            k = 6 if rs_item(right, 6)[1] == j else 5
            got(rs_key(right, k))
            total += rs_r[0 if right else 1, k].astype(F32)
        grad = (total * slope_map[pl.ds(j * HALF, HALF), :]).astype(BF)
        xp[pl.ds(32 + j * HALF, HALF), :] = grad
        dm[8 * j:8 * j + 8] = grad.reshape(8, 32, CH)
        xf[8 * j:8 * j + 8] = grad.astype(F32).reshape(8, 32, CH)
    scol[1, 0] = xf[:, 31, :].astype(BF)
    scol[1, 1] = xf[:, 0, :].astype(BF)
    halo_send(1, dm)
    ar4(1)
    ar4(0)
    halo_recv(1)
    ar5(1)
    ar5(0)
    for j in range(2):
        gmap_ref[8 * j:8 * j + 8] = conv_map(twt, j).astype(BF).reshape(8, 32, CH)
    ar6(1)
    ar6(0)
    ar7(1)
    ar7(0)
    got(K_AR + 27)
    got(K_AR + AR_N + 27)
    for k in sorted(live):
        live[k].wait_send()


def step(in_map, tile_w, head_w1, head_w2, box_row, box_col, box_target, head_cot):
    vm = pltpu.VMEM
    scratch = [
        vm((16, 32, CH), F32),
        vm((576, CH), BF),
        vm((576, 3 * CH), BF),
        vm((PX, CH), F32),
        vm((2, 2, 16, CH), BF),
        vm((2, 2, 32, CH), BF),
        vm((2, 6, 16, CH), BF),
        vm((24, CH), F32),
        vm((24, CH), F32),
        vm((NZ, 16, 128), jnp.int32),
        vm((4, POS, 128), jnp.int32),
        vm((1, 4 * POS), jnp.int32),
        vm((NZ, PX, CH), BF),
        vm((4, POS, CH), F32),
        vm((1056, 3 * CH), BF),
        vm((1056, 3 * CH), BF),
        vm((1056, 3 * CH), BF),
        vm((1056, 3 * CH), BF),
        vm((4, 224, CH), F32),
        vm((14, 16, CH), F32),
        vm((CH, 4 * POS), BF),
        vm((3, 3 * CH, CH), BF),
        vm((3, 3 * CH, CH), BF),
        vm((3, 3 * CH, CH), BF),
        vm((4 * POS, CH), BF),
        vm((2, 7, HALF, CH), BF),
        vm((2, 7, HALF, CH), BF),
        vm((16, 32, CH), BF),
        vm((2, 9, 256, 128), F32),
        vm((2, 9, 256, 128), BF),
        vm((2, 9, 256, 128), BF),
        vm((2, 9, 256, 128), BF),
        vm((2, 3, 9, 64, 128), BF),
        vm((2, 9, 64, 128), F32),
        vm((2, 9, 64, 128), BF),
        vm((2, 3, 9, 16, 128), BF),
        vm((2, 16, 16, 128), F32),
        vm((2, 16, 16, 128), BF),
        vm((2, 7, 2, 16, 128), BF),
        vm((2, 16, 16, 128), BF),
        pltpu.SemaphoreType.DMA((N_SEM,)),
        pltpu.SemaphoreType.DMA((N_SEM,)),
    ]
    in_vmem = pl.BlockSpec(memory_space=pltpu.VMEM)
    grad_map, sums = pl.pallas_call(
        kernel,
        out_shape=(
            jax.ShapeDtypeStruct((16, 32, CH), BF),
            jax.ShapeDtypeStruct((2, 2, 9, 256, 128), BF),
        ),
        in_specs=[in_vmem] * 8,
        out_specs=(in_vmem, in_vmem),
        scratch_shapes=scratch,
        compiler_params=pltpu.CompilerParams(
            collective_id=0, has_side_effects=True, vmem_limit_bytes=58 * 1024 * 1024
        ),
        cost_estimate=pl.CostEstimate(flops=8 * 10**9, bytes_accessed=10**7, transcendentals=10**6),
    )(
        in_map,
        tile_w.reshape(3, 3 * CH, CH),
        head_w1.reshape(3, 3 * CH, CH),
        head_w2.reshape(3, 3 * CH, CH),
        box_row,
        box_col,
        box_target,
        head_cot,
    )
    factor = 1.0 / math.sqrt(32 * 8 * 4 * 14 * 14)
    sums = sums.transpose(0, 2, 3, 1, 4).astype(F32) * factor
    sums = sums.reshape(2, 3, 3, CH, CH)
    return grad_map, sums[0], sums[1]


def solution(mesh):
    in_specs = (
        P("row", "col", None),
        P(),
        P(),
        P(),
        P("row", "col"),
        P("row", "col"),
        P("row", "col"),
        P("row", "col", None, None, None),
    )
    out_specs = (P("row", "col", None), P(), P())
    return jax.shard_map(step, mesh=mesh, in_specs=in_specs, out_specs=out_specs, check_vma=False)
```

time: 491 us -> 128 us (0.26)
  waiting for transfers between devices: 222 us -> 0 us
  Pallas kernels: 0 us -> 108 us
  local copies, waits for them, and re-layouts: 104 us -> 17.2 us
  loops' own time: 63.1 us -> 0 us
  starting transfers between devices: 38 us -> 0 us
  matrix products: 30.9 us -> 0 us
  between operations: 14.8 us -> 0.67 us
  other arithmetic: 13.8 us -> 2.22 us
    psum x1 -> x0, waiting for transfers between devices: 153 us -> none  [body(): lax.psum((first_local, second_local), ('row', 'col'))]
    pallas_call x0 -> x1, Pallas kernels: none -> 108 us  [step(): pl.pallas_call(kernel, out_shape=(jax.ShapeDtypeStruct((16, 32, CH), BF),...]
    another operation x2 -> x0, loops' own time: 63.1 us -> none  [the longest x1 62.9 us: body(): lax.fori_loop(0, slot_count, add_box, jnp.zeros((tile_rows, tile_cols, ch...]
    all_to_all x3 -> x0, waiting for transfers between devices: 62.9 us -> none  [the longest x1 38 us: body(): lax.all_to_all(outgoing, 'col', split_axis=0, concat_axis=0, tiled=True)]
    gather x64 -> x0, local copies, waits for them, and re-layouts: 41.8 us -> none
    dot_general x23 -> x0, matrix products: 23.9 us -> none  [the longest x18 18.9 us: weight_grad(): lax.dot_general(window, flat_delta, (((0,), (0,)), ((), ())), preferred_e...]
    ppermute x8 -> x0, starting transfers between devices: 22 us -> none  [the longest x4 12.4 us: padded_2(): before = lax.ppermute(last, axis, up)]
    reshape x13 -> x0, local copies, waits for them, and re-layouts: 21.5 us -> none  [the longest x2 6.28 us: body(): pick_rows(send_map, crops)]
  transfers between devices with their start and end apart: 12 -> 0, of which waited for: 6 -> 0; matrix products, arithmetic and copies ran while one was open for 13% -> 0% of each run, Pallas kernels for 0% -> 0%
where the time goes in v1:
time: 128 us
  Pallas kernels  108 us (84%)
  local copies, waits for them, and re-layouts  17.2 us (13%)
  other arithmetic  2.22 us (2%)
    pallas_call x1, Pallas kernels, step(): pl.pallas_call(kernel, out_shape=(jax.ShapeDtypeStruct((16, 32, CH), BF),...  108 us
    unnamed x9, local copies, waits for them, and re-layouts  10.4 us
    slice x3, local copies, waits for them, and re-layouts, step(): return (grad_map, sums[0], sums[1])  6.76 us

profile of v1, /device:TPU:1, one launch (start us, length us, event | category | flops | bytes accessed | tf_op | source)
XLA Modules:
  0.0 128.0 jit_solution(17957498362831657646)
XLA Ops:
  0.6 1.3 %copy.15.brow_ref = s32[16,1]{1,0:T(8,128)} copy(s32[16,1]{0,1:T(1,128)} %param.12) | data formatting | bytes 128 | tf_op args[4]
  2.0 1.3 %copy.16.bcol_ref = s32[16,1]{1,0:T(8,128)} copy(s32[16,1]{0,1:T(1,128)} %param.13) | data formatting | bytes 128 | tf_op args[5]
  3.3 1.3 %copy.17.btgt_ref = s32[16,1]{1,0:T(8,128)} copy(s32[16,1]{0,1:T(1,128)} %param.14) | data formatting | bytes 128 | tf_op args[6]
  4.6 1.8 %copy.18.cot_ref = bf16[4,1,14,14,256]{4,3,2,1,0:T(8,128)(2,1)} copy(bf16[4,1,14,14,256]{4,0,3,2,1:T(4,128)(2,1)} %param.15) | data formatting | bytes 802816 | tf_op args[7]
  6.4 107.9 %shard_map.103 = (bf16[16,32,256]{2,1,0:T(8,128)(2,1)}, bf16[2,2,9,256,128]{4,3,2,1,0:T(8,128)(2,1)}) custom-call(bf16[16,32,256]{2,1,0:T(8,128)(2,1)} %in_ref.1, bf16[3,768,256]{2,1,0:T(8,128)(2,1)} %bitcast.9, bf16[3,768,256]{2,1,0:T(8,128)(2,1)} %bitcast.10, bf16[3,768,256]{2,1,0:T(8,128)(2,1)} %bitcast.11, s32[16,1]{1,0:T(8,128)} %copy.15.brow_ref, ...), custom_call_target="tpu_custom_call" | custom-call | flops 8000000000 | bytes 10000000 | tf_op jit(solution)/shard_map/pallas_call | solution.py:503
  114.4 2.2 %multiply_bitcast_fusion = f32[2,9,256,2,128]{4,2,1,3,0:T(8,128)S(1)} fusion(bf16[2,2,9,256,128]{4,3,2,1,0:T(8,128)(2,1)} %get-tuple-element.6), kind=kLoop, calls=%fused_computation | loop fusion | flops 2359296 | bytes 7077888 | tf_op jit(solution)/shard_map/mul | solution.py:527
  116.6 2.7 %fusion = (f32[1,9,256,2,128]{4,2,1,3,0:T(8,128)}, f32[1,9,256,2,128]{4,2,1,3,0:T(8,128)}) fusion(f32[2,9,256,2,128]{4,2,1,3,0:T(8,128)S(1)} %multiply_bitcast_fusion), kind=kLoop, calls=%fused_computation.1 | loop fusion | bytes 9437184 | tf_op jit(solution)/shard_map/slice | solution.py:529
  119.3 2.0 %copy.20 = f32[1,9,256,2,128]{2,4,3,1,0:T(8,128)S(1)} copy(f32[1,9,256,2,128]{4,2,1,3,0:T(8,128)} %get-tuple-element.10) | data formatting | bytes 4718592 | tf_op jit(solution)/shard_map/slice | solution.py:529
  121.3 2.0 %copy.22 = f32[3,3,256,256]{3,2,1,0:T(8,128)} copy(f32[3,3,256,256]{2,3,1,0:T(8,128)S(1)} %bitcast.7) | data formatting | bytes 4718592
  123.3 2.0 %copy.19 = f32[1,9,256,2,128]{2,4,3,1,0:T(8,128)S(1)} copy(f32[1,9,256,2,128]{4,2,1,3,0:T(8,128)} %get-tuple-element.11) | data formatting | bytes 4718592 | tf_op jit(solution)/shard_map/slice | solution.py:529
  125.3 0.0 copy-start
  125.4 2.0 %copy.21 = f32[3,3,256,256]{3,2,1,0:T(8,128)} copy(f32[3,3,256,256]{2,3,1,0:T(8,128)S(1)} %bitcast.8) | data formatting | bytes 4718592
  127.3 0.0 copy-done
  127.3 0.7 copy.24
Async XLA Ops:
  125.3 2.0 %copy-start = (bf16[16,32,256]{2,1,0:T(8,128)(2,1)S(1)}, bf16[16,32,256]{2,1,0:T(8,128)(2,1)}, u32[]{:S(2)}) copy-start(bf16[16,32,256]{2,1,0:T(8,128)(2,1)} %get-tuple-element.15) | copy-start | bytes 786436

commit v2 on v1

--- a/solution.py
+++ b/solution.py
@@ -24,7 +24,8 @@
 K_RS = 37
 K_AR = 51
 AR_N = 28
-N_SEM = K_AR + 2 * AR_N
+N_SEM = K_AR + 4 * AR_N
+PARTS = ((1, 0, 5, False), (1, 5, 4, True), (0, 0, 5, True), (0, 5, 4, False))
 
 
 def silu_slope(values):
@@ -40,7 +41,7 @@
     in_ref, tw_ref, w1_ref, w2_ref, brow_ref, bcol_ref, btgt_ref, cot_ref,
     gmap_ref, gsum_ref,
     xf, xp, x3m, slope_map, scol, hrow, hcol, hl, hr,
-    tab, gcol, grow, feats, acc, xc3, xh3, d23, d13, slope1, cotp, xt,
+    tab, gcol, grow, feats, acc, xc3, xh3, d23, d13, slope1, cotf, cots, xt,
     twt, w1t, w2t, bg, rs_s, rs_r, dm,
     own, snd, rc, s1, r1, t2, s2, r2, t3, s3, r3, zb,
     ssem, rsem,
@@ -90,10 +91,12 @@
     xf[...] = in_ref[...].astype(F32)
     scol[0, 0] = xf[:, 31, :].astype(BF)
     scol[0, 1] = xf[:, 0, :].astype(BF)
-    code = btgt_ref[...] * 128 + brow_ref[...] * 32 + bcol_ref[...]
-    tab[0] = jnp.broadcast_to(code, (16, 128))
+    tab[0] = jnp.full((8, 128), -128, jnp.int32)
+    tab[0, 0:1, 0:16] = btgt_ref[...] * 128 + brow_ref[...] * 32 + bcol_ref[...]
     for buf in (xc3, xh3, d23, d13):
-        buf[...] = jnp.zeros_like(buf)
+        for h in range(5):
+            at = max(h * POS, 0)
+            buf[at:at + 32, :] = jnp.zeros((32, 3 * CH), BF)
     acc[...] = jnp.zeros_like(acc)
     xp[pl.ds(32, PX), :] = in_ref[...].reshape(PX, CH)
 
@@ -145,18 +148,15 @@
         total += mm(x3m[pl.ds(j * HALF + 64, HALF), :], w[2])
         return total
 
-    def turn(src, dst):
-        def one(a, carry):
+    def turn(src, dst, taps):
+        for a in taps:
             for b in range(3):
                 dst[a, b * CH:(b + 1) * CH, :] = src[2 - a, (2 - b) * CH:(3 - b) * CH, :].T
-            return carry
-
-        lax.fori_loop(0, 3, one, 0)
 
     halo_send(0, in_ref)
     for d in range(1, NZ):
         send(tab.at[0], tab.at[d], K_TAB + d - 1, at_z(d))
-    turn(w2_ref, w2t)
+    turn(w2_ref, w2t, (0, 1, 2))
     halo_recv(0)
 
     def ag_key(right, s, j):
@@ -177,13 +177,13 @@
     for d in range(1, NZ):
         got(K_TAB + d - 1)
     for h in range(4):
-        base = jnp.zeros((1, 128), jnp.int32)
+        base = jnp.zeros((1, 1), jnp.int32)
         for s in range(NZ):
             tile = lax.rem(me - s + NZ, NZ)
-            word = tab[s]
+            word = tab[s, 0:1, :]
             hit = (word >> 7) == me * 4 + h
             value = (word & 127) + tile * PX
-            base += jnp.sum(jnp.where(hit, value, 0), axis=0, keepdims=True)
+            base += jnp.sum(jnp.where(hit, value, 0), axis=1, keepdims=True)
         p = lax.broadcasted_iota(jnp.int32, (POS, 128), 0)
         i, j = p >> 4, p & 15
         ok = (i >= 1) & (i <= 14) & (j < 14)
@@ -191,8 +191,7 @@
         p = lax.broadcasted_iota(jnp.int32, (1, POS), 1)
         i, j = p >> 4, p & 15
         ok = (i >= 1) & (i <= 14) & (j < 14)
-        both = jnp.concatenate([base, base], axis=1)
-        grow[0:1, h * POS:(h + 1) * POS] = jnp.where(ok, both + (i - 1) * 32 + j, -1)
+        grow[0:1, h * POS:(h + 1) * POS] = jnp.where(ok, base + (i - 1) * 32 + j, -1)
 
     def take(s, j):
         tile = lax.rem(me - s + NZ, NZ)
@@ -211,6 +210,15 @@
 
     take(0, 0)
     take(0, 1)
+
+    def spread(i, carry):
+        cotf[...] = cot_ref[i].astype(F32)
+        for h in range(4):
+            cots[h, i, 0:14, :] = cotf[:, h, :]
+            cots[h, i, 14:16, :] = jnp.zeros((2, CH), F32)
+        return carry
+
+    lax.fori_loop(0, 14, spread, 0)
     for s in range(1, 4):
         for j in range(2):
             got(ag_key(True, s - 1, j))
@@ -221,10 +229,11 @@
                 ag_send(False, s, j)
             take(s, j)
             take(NZ - s, j)
-            if s == 1 and j == 0:
-                turn(w1_ref, w1t)
-            if s == 1 and j == 1:
-                turn(tw_ref, twt)
+            if s < 3:
+                n = 2 * (s - 1) + j
+                if n < 3:
+                    turn(w1_ref, w1t, (n,))
+                turn(tw_ref, twt, (n,) if n < 3 else ())
     got(ag_key(True, 3, 0))
     take(4, 0)
     got(ag_key(False, 3, 1))
@@ -233,7 +242,7 @@
     inside = (lax.broadcasted_iota(jnp.int32, (224, CH), 0) & 15) < 14
 
     def put(buf, h, value):
-        at = pl.multiple_of(h * POS + 32, 16)
+        at = h * POS + 32
         mid = value.astype(BF)
         full = mid.astype(F32)
         buf[pl.ds(at, 224), 0:CH] = pltpu.roll(full, 1, 0).astype(BF)
@@ -241,7 +250,7 @@
         buf[pl.ds(at, 224), 2 * CH:3 * CH] = pltpu.roll(full, 223, 0).astype(BF)
 
     def conv_box(buf, w, h):
-        at = pl.multiple_of(h * POS + 16, 16)
+        at = h * POS + 16
         total = mm(buf[pl.ds(at, 224), :], w[0])
         total += mm(buf[pl.ds(at + 16, 224), :], w[1])
         total += mm(buf[pl.ds(at + 32, 224), :], w[2])
@@ -250,23 +259,15 @@
     def cut(v):
         return jnp.where(inside, v, 0.0)
 
-    def chain(h, carry):
+    for h in range(4):
         put(xc3, h, acc[h, 16:240, :])
-        pre_one = conv_box(xc3, w1_ref, h)
-        put(xh3, h, cut(pre_one * jax.nn.sigmoid(pre_one)))
-        slope1[h] = silu_slope(pre_one)
-        pre_two = conv_box(xh3, w2_ref, h)
-        cotp[:, 0:14, :] = cot_ref[h, 0].astype(F32)
-        cotp[:, 14:16, :] = jnp.zeros((14, 2, CH), F32)
-        put(d23, h, cut(cotp[...].reshape(224, CH) * silu_slope(pre_two)))
-        put(d13, h, cut(conv_box(d23, w2t, h) * slope1[h]))
-        at = pl.multiple_of(h * POS, 16)
-        bg[pl.ds(at, 16), :] = jnp.zeros((16, CH), BF)
-        bg[pl.ds(at + 240, 16), :] = jnp.zeros((16, CH), BF)
-        bg[pl.ds(at + 16, 224), :] = conv_box(d13, w1t, h).astype(BF)
-        return carry
-
-    lax.fori_loop(0, 4, chain, 0)
+    for h in range(4):
+        pre = conv_box(xc3, w1_ref, h)
+        put(xh3, h, cut(pre * jax.nn.sigmoid(pre)))
+        slope1[h] = silu_slope(pre)
+    for h in range(4):
+        pre = conv_box(xh3, w2_ref, h)
+        put(d23, h, cut(cots[h].reshape(224, CH) * silu_slope(pre)))
 
     def term(d, j):
         tile = lax.rem(me + d + NZ, NZ)
@@ -310,16 +311,20 @@
             return carry
 
         lax.fori_loop(0, 3, one, 0)
-        send(snd.at[g], rc.at[g], K_AR + g * AR_N, sibling)
-
-    def axes(g):
-        if g == 0:
+        for n in (2 * (1 - g), 2 * (1 - g) + 1):
+            t0, nt = PARTS[n][1:3]
+            span = pl.ds(t0, nt)
+            send(snd.at[g, span], rc.at[g, span], K_AR + n * AR_N, sibling)
+
+    def axes(n):
+        if PARTS[n][3]:
             return at_x, px, NX, at_y, py, NY
         return at_y, py, NY, at_x, px, NX
 
-    def ar1(g):
-        k = K_AR + g * AR_N
-        at1, p1, n1 = axes(g)[:3]
+    def ar1(n):
+        g, t0, nt, _ = PARTS[n]
+        k = K_AR + n * AR_N
+        at1, p1, n1 = axes(n)[:3]
         got(k)
 
         def one(t, carry):
@@ -328,100 +333,119 @@
             s1[g, t] = v.astype(BF)
             return carry
 
-        lax.fori_loop(0, 9, one, 0)
+        lax.fori_loop(t0, t0 + nt, one, 0)
         for d in range(1, 4):
             q = lax.rem(p1 + d, n1)
-            send(s1.at[g, :, pl.ds(q * 64, 64), :], r1.at[g, d - 1], k + d, at1(d))
-
-    def ar2(g):
-        k = K_AR + g * AR_N
-        at1, p1, n1, at2, p2, n2 = axes(g)
+            src = s1.at[g, pl.ds(t0, nt), pl.ds(q * 64, 64), :]
+            send(src, r1.at[n, d - 1, pl.ds(0, nt)], k + d, at1(d))
+
+    def ar2(n):
+        g, t0, nt, _ = PARTS[n]
+        k = K_AR + n * AR_N
+        at1, p1, n1, at2, p2, n2 = axes(n)
         for d in range(1, 4):
             got(k + d)
 
         def one(t, carry):
-            v = own[g, t, pl.ds(p1 * 64, 64), :]
+            v = own[g, t0 + t, pl.ds(p1 * 64, 64), :]
             for d in range(3):
-                v += r1[g, d, t].astype(F32)
-            t2[g, t] = v
-            s2[g, t] = v.astype(BF)
+                v += r1[n, d, t].astype(F32)
+            t2[n, t] = v
+            s2[n, t] = v.astype(BF)
             return carry
 
-        lax.fori_loop(0, 9, one, 0)
+        lax.fori_loop(0, nt, one, 0)
         for d in range(1, 4):
             q = lax.rem(p2 + d, n2)
-            send(s2.at[g, :, pl.ds(q * 16, 16), :], r2.at[g, d - 1], k + 3 + d, at2(d))
-
-    def ar3(g):
-        k = K_AR + g * AR_N
-        p2 = axes(g)[4]
+            src = s2.at[n, pl.ds(0, nt), pl.ds(q * 16, 16), :]
+            send(src, r2.at[n, d - 1, pl.ds(0, nt)], k + 3 + d, at2(d))
+
+    def ar3(n):
+        nt = PARTS[n][2]
+        k = K_AR + n * AR_N
+        p2 = axes(n)[4]
         for d in range(1, 4):
             got(k + 3 + d)
-        v = t2[g, :, pl.ds(p2 * 16, 16), :]
+        v = t2[n, 0:nt, pl.ds(p2 * 16, 16), :]
         for d in range(3):
-            v += r2[g, d].astype(F32)
-        t3[g, 0:9] = v
-        t3[g, 9:16] = jnp.zeros((7, 16, 128), F32)
-        s3[g, 0:9] = v.astype(BF)
-        s3[g, 9:16] = jnp.zeros((7, 16, 128), BF)
+            v += r2[n, d, 0:nt].astype(F32)
+        t3[n, 0:nt] = v
+        t3[n, nt:8] = jnp.zeros((8 - nt, 16, 128), F32)
+        s3[n, 0:nt] = v.astype(BF)
+        s3[n, nt:8] = jnp.zeros((8 - nt, 16, 128), BF)
         for d in range(1, NZ):
             q = lax.rem(me + d, NZ)
-            send(s3.at[g, pl.ds(q * 2, 2)], r3.at[g, d - 1], k + 6 + d, at_z(d))
-
-    def ar4(g):
-        k = K_AR + g * AR_N
+            send(s3.at[n, q], r3.at[n, d - 1], k + 6 + d, at_z(d))
+
+    def ar4(n):
+        k = K_AR + n * AR_N
         for d in range(1, NZ):
             got(k + 6 + d)
-        v = t3[g, pl.ds(me * 2, 2)]
+        v = t3[n, me]
         for d in range(NZ - 1):
-            v += r3[g, d].astype(F32)
-        zb[g, pl.ds(me * 2, 2)] = v.astype(BF)
+            v += r3[n, d].astype(F32)
+        zb[n, me] = v.astype(BF)
         for d in range(1, NZ):
-            part = zb.at[g, pl.ds(me * 2, 2)]
-            send(part, part, k + 13 + d, at_z(d))
-
-    def ar5(g):
-        k = K_AR + g * AR_N
-        at1, p1, n1, at2, p2, n2 = axes(g)
+            send(zb.at[n, me], zb.at[n, me], k + 13 + d, at_z(d))
+
+    def ar5(n):
+        g, t0, nt, _ = PARTS[n]
+        k = K_AR + n * AR_N
+        at1, p1, n1, at2, p2, n2 = axes(n)
         for d in range(1, NZ):
             got(k + 13 + d)
         at = pl.multiple_of(p1 * 64 + p2 * 16, 16)
-        gsum_ref[g, core, :, pl.ds(at, 16), :] = zb[g, 0:9]
-        part = gsum_ref.at[g, core, :, pl.ds(at, 16), :]
+        gsum_ref[g, core, t0:t0 + nt, pl.ds(at, 16), :] = zb[n, 0:nt]
+        part = gsum_ref.at[g, core, pl.ds(t0, nt), pl.ds(at, 16), :]
         for d in range(1, 4):
             send(part, part, k + 20 + d, at2(d))
 
-    def ar6(g):
-        k = K_AR + g * AR_N
-        at1, p1, n1 = axes(g)[:3]
+    def ar6(n):
+        g, t0, nt, _ = PARTS[n]
+        k = K_AR + n * AR_N
+        at1, p1, n1 = axes(n)[:3]
         for d in range(1, 4):
             got(k + 20 + d)
-        part = gsum_ref.at[g, core, :, pl.ds(p1 * 64, 64), :]
+        part = gsum_ref.at[g, core, pl.ds(t0, nt), pl.ds(p1 * 64, 64), :]
         for d in range(1, 4):
             send(part, part, k + 23 + d, at1(d))
 
-    def ar7(g):
-        k = K_AR + g * AR_N
+    def ar7(n):
+        g, t0, nt, _ = PARTS[n]
+        k = K_AR + n * AR_N
         for d in range(1, 4):
             got(k + 23 + d)
-        part = gsum_ref.at[g, core]
+        part = gsum_ref.at[g, core, pl.ds(t0, nt)]
         send(part, part, k + 27, sibling)
 
+    def both(stage, g):
+        stage(2 * (1 - g))
+        stage(2 * (1 - g) + 1)
+
+    wgrad(1, xh3, d23)
+    for h in range(4):
+        put(d13, h, cut(conv_box(d23, w2t, h) * slope1[h]))
+    for h in range(4):
+        bg[h * POS:h * POS + 16, :] = jnp.zeros((16, CH), BF)
+        bg[h * POS + 240:(h + 1) * POS, :] = jnp.zeros((16, CH), BF)
+        bg[h * POS + 16:h * POS + 240, :] = conv_box(d13, w1t, h).astype(BF)
     rs_step(0)
+    both(ar1, 1)
     rs_step(1)
-    wgrad(1, xh3, d23)
+    wgrad(0, xc3, d13)
     rs_step(2)
-    wgrad(0, xc3, d13)
+    both(ar1, 0)
     rs_step(3)
-    ar1(1)
-    ar1(0)
+    both(ar2, 1)
     rs_step(4)
+    both(ar2, 0)
+    both(ar3, 1)
     rs_step(5)
-    ar2(1)
-    ar2(0)
+    both(ar3, 0)
+    both(ar4, 1)
     rs_step(6)
-    ar3(1)
-    ar3(0)
+    both(ar4, 0)
+    both(ar5, 1)
 
     for j in range(2):
         total = term(0, j)
@@ -436,21 +460,26 @@
     scol[1, 0] = xf[:, 31, :].astype(BF)
     scol[1, 1] = xf[:, 0, :].astype(BF)
     halo_send(1, dm)
-    ar4(1)
-    ar4(0)
+    both(ar5, 0)
+    both(ar6, 1)
     halo_recv(1)
-    ar5(1)
-    ar5(0)
     for j in range(2):
         gmap_ref[8 * j:8 * j + 8] = conv_map(twt, j).astype(BF).reshape(8, 32, CH)
-    ar6(1)
-    ar6(0)
-    ar7(1)
-    ar7(0)
-    got(K_AR + 27)
-    got(K_AR + AR_N + 27)
+    both(ar6, 0)
+    both(ar7, 1)
+    both(ar7, 0)
+    for n in range(4):
+        got(K_AR + n * AR_N + 27)
     for k in sorted(live):
         live[k].wait_send()
+
+
+def finish(map_ref, sums_ref, out_ref, first_ref, second_ref):
+    factor = 1.0 / math.sqrt(32 * 8 * 4 * 14 * 14)
+    out_ref[...] = map_ref[...]
+    for g, ref in enumerate((first_ref, second_ref)):
+        for half in range(2):
+            ref[:, :, half * 128:half * 128 + 128] = sums_ref[g, half].astype(F32) * factor
 
 
 def step(in_map, tile_w, head_w1, head_w2, box_row, box_col, box_target, head_cot):
@@ -465,7 +494,7 @@
         vm((2, 6, 16, CH), BF),
         vm((24, CH), F32),
         vm((24, CH), F32),
-        vm((NZ, 16, 128), jnp.int32),
+        vm((NZ, 8, 128), jnp.int32),
         vm((4, POS, 128), jnp.int32),
         vm((1, 4 * POS), jnp.int32),
         vm((NZ, PX, CH), BF),
@@ -475,7 +504,8 @@
         vm((1056, 3 * CH), BF),
         vm((1056, 3 * CH), BF),
         vm((4, 224, CH), F32),
-        vm((14, 16, CH), F32),
+        vm((14, 4, CH), F32),
+        vm((4, 14, 16, CH), F32),
         vm((CH, 4 * POS), BF),
         vm((3, 3 * CH, CH), BF),
         vm((3, 3 * CH, CH), BF),
@@ -488,14 +518,14 @@
         vm((2, 9, 256, 128), BF),
         vm((2, 9, 256, 128), BF),
         vm((2, 9, 256, 128), BF),
-        vm((2, 3, 9, 64, 128), BF),
-        vm((2, 9, 64, 128), F32),
-        vm((2, 9, 64, 128), BF),
-        vm((2, 3, 9, 16, 128), BF),
-        vm((2, 16, 16, 128), F32),
-        vm((2, 16, 16, 128), BF),
-        vm((2, 7, 2, 16, 128), BF),
-        vm((2, 16, 16, 128), BF),
+        vm((4, 3, 5, 64, 128), BF),
+        vm((4, 5, 64, 128), F32),
+        vm((4, 5, 64, 128), BF),
+        vm((4, 3, 5, 16, 128), BF),
+        vm((4, NZ, 16, 128), F32),
+        vm((4, NZ, 16, 128), BF),
+        vm((4, 7, 16, 128), BF),
+        vm((4, NZ, 16, 128), BF),
         pltpu.SemaphoreType.DMA((N_SEM,)),
         pltpu.SemaphoreType.DMA((N_SEM,)),
     ]
@@ -518,15 +548,30 @@
         tile_w.reshape(3, 3 * CH, CH),
         head_w1.reshape(3, 3 * CH, CH),
         head_w2.reshape(3, 3 * CH, CH),
-        box_row,
-        box_col,
-        box_target,
-        head_cot,
+        box_row.T,
+        box_col.T,
+        box_target.T,
+        head_cot[:, 0].transpose(1, 2, 0, 3),
     )
-    factor = 1.0 / math.sqrt(32 * 8 * 4 * 14 * 14)
-    sums = sums.transpose(0, 2, 3, 1, 4).astype(F32) * factor
-    sums = sums.reshape(2, 3, 3, CH, CH)
-    return grad_map, sums[0], sums[1]
+    grad_map, first, second = pl.pallas_call(
+        finish,
+        grid=(3,),
+        out_shape=(
+            jax.ShapeDtypeStruct((16, 32, CH), BF),
+            jax.ShapeDtypeStruct((9, CH, CH), F32),
+            jax.ShapeDtypeStruct((9, CH, CH), F32),
+        ),
+        in_specs=[
+            pl.BlockSpec((16, 32, CH), lambda i: (0, 0, 0)),
+            pl.BlockSpec((2, 2, 3, CH, 128), lambda i: (0, 0, i, 0, 0)),
+        ],
+        out_specs=(
+            pl.BlockSpec((16, 32, CH), lambda i: (0, 0, 0)),
+            pl.BlockSpec((3, CH, CH), lambda i: (i, 0, 0)),
+            pl.BlockSpec((3, CH, CH), lambda i: (i, 0, 0)),
+        ),
+    )(grad_map, sums)
+    return grad_map, first.reshape(3, 3, CH, CH), second.reshape(3, 3, CH, CH)
 
 
 def solution(mesh):

time: 128 us -> 101 us (0.79)
  local copies, waits for them, and re-layouts: 17.2 us -> 0 us
  Pallas kernels: 108 us -> 101 us
  other arithmetic: 2.22 us -> 0 us
    pallas_call x1, Pallas kernels: 108 us -> 96.2 us  [step(): pl.pallas_call(kernel, out_shape=(jax.ShapeDtypeStruct((16, 32, CH), BF),...]
    unnamed x9 -> x0, local copies, waits for them, and re-layouts: 10.4 us -> none
    slice x3 -> x0, local copies, waits for them, and re-layouts: 6.76 us -> none  [step(): return (grad_map, sums[0], sums[1])]
    pallas_call x0 -> x1, Pallas kernels: none -> 4.42 us  [step(): pl.pallas_call(finish, grid=(3,), out_shape=(jax.ShapeDtypeStruct((16, 32...]
    mul x1 -> x0, other arithmetic: 2.22 us -> none  [step(): sums = sums.transpose(0, 2, 3, 1, 4).astype(F32) * factor]
where the time goes in v2:
time: 101 us
  Pallas kernels  101 us (100%)
    pallas_call x1, Pallas kernels, step(): pl.pallas_call(kernel, out_shape=(jax.ShapeDtypeStruct((16, 32, CH), BF),...  96.2 us
    pallas_call x1, Pallas kernels, step(): pl.pallas_call(finish, grid=(3,), out_shape=(jax.ShapeDtypeStruct((16, 32...  4.42 us

profile of v2, /device:TPU:1, one launch (start us, length us, event | category | flops | bytes accessed | tf_op | source)
XLA Modules:
  0.0 101.3 jit_solution(16964737818517653298)
XLA Ops:
  0.6 96.2 %shard_map.103 = (bf16[16,32,256]{2,1,0:T(8,128)(2,1)}, bf16[2,2,9,256,128]{4,3,2,1,0:T(8,128)(2,1)}) custom-call(bf16[16,32,256]{2,1,0:T(8,128)(2,1)} %in_ref.1, bf16[3,768,256]{2,1,0:T(8,128)(2,1)} %bitcast.13, bf16[3,768,256]{2,1,0:T(8,128)(2,1)} %bitcast.14, bf16[3,768,256]{2,1,0:T(8,128)(2,1)} %bitcast.15, s32[1,16]{1,0:T(1,128)} %bitcast.17, ...), custom_call_target="tpu_custom_call" | custom-call | flops 8000000000 | bytes 10000000 | tf_op jit(solution)/shard_map/pallas_call | solution.py:533
  96.9 4.4 %shard_map.104 = (bf16[16,32,256]{2,1,0:T(8,128)(2,1)}, f32[9,256,256]{2,1,0:T(8,128)}, f32[9,256,256]{2,1,0:T(8,128)}) custom-call(bf16[16,32,256]{2,1,0:T(8,128)(2,1)} %get-tuple-element.8.map_ref, bf16[2,2,9,256,128]{4,3,2,1,0:T(8,128)(2,1)} %get-tuple-element.9.sums_ref), custom_call_target="tpu_custom_call" | custom-call | tf_op jit(solution)/shard_map/pallas_call | solution.py:556

commit v3 on v2

--- a/solution.py
+++ b/solution.py
@@ -23,7 +23,7 @@
 K_AG = 23
 K_RS = 37
 K_AR = 51
-AR_N = 28
+AR_N = 33
 N_SEM = K_AR + 4 * AR_N
 PARTS = ((1, 0, 5, False), (1, 5, 4, True), (0, 0, 5, True), (0, 5, 4, False))
 
@@ -38,13 +38,13 @@
 
 
 def kernel(
-    in_ref, tw_ref, w1_ref, w2_ref, brow_ref, bcol_ref, btgt_ref, cot_ref,
+    in_ref, tw_any, w1_any, w2_any, brow_ref, bcol_ref, btgt_ref, cot_any,
     gmap_ref, gsum_ref,
-    xf, xp, x3m, slope_map, scol, hrow, hcol, hl, hr,
+    tw_ref, w1_ref, w2_ref, cot_ref, xf, xp, x3m, slope_map, scol, hrow, hcol, hl, hr,
     tab, gcol, grow, feats, acc, xc3, xh3, d23, d13, slope1, cotf, cots, xt,
     twt, w1t, w2t, bg, rs_s, rs_r, dm,
     own, snd, rc, s1, r1, t2, s2, r2, t3, s3, r3, zb,
-    ssem, rsem,
+    ssem, rsem, lsem,
 ):
     row = lax.axis_index("row")
     me = lax.axis_index("col")
@@ -88,16 +88,18 @@
     for dev in partners:
         pl.semaphore_signal(barrier, inc=1, device_id=dev, device_id_type=MESH)
 
+    loads = []
+    for n, (src, dst) in enumerate(
+        ((tw_any, tw_ref), (w2_any, w2_ref), (w1_any, w1_ref), (cot_any, cot_ref))
+    ):
+        loads.append(pltpu.make_async_copy(src, dst, lsem.at[n]))
+        loads[n].start()
+
     xf[...] = in_ref[...].astype(F32)
     scol[0, 0] = xf[:, 31, :].astype(BF)
     scol[0, 1] = xf[:, 0, :].astype(BF)
     tab[0] = jnp.full((8, 128), -128, jnp.int32)
     tab[0, 0:1, 0:16] = btgt_ref[...] * 128 + brow_ref[...] * 32 + bcol_ref[...]
-    for buf in (xc3, xh3, d23, d13):
-        for h in range(5):
-            at = max(h * POS, 0)
-            buf[at:at + 32, :] = jnp.zeros((32, 3 * CH), BF)
-    acc[...] = jnp.zeros_like(acc)
     xp[pl.ds(32, PX), :] = in_ref[...].reshape(PX, CH)
 
     pl.semaphore_wait(barrier, len(partners))
@@ -140,7 +142,7 @@
             x3m[pl.ds(at, 32), 2 * CH:3 * CH] = rt.astype(BF)
             return carry
 
-        lax.fori_loop(0, 18, one, 0)
+        return one
 
     def conv_map(w, j):
         total = mm(x3m[pl.ds(j * HALF, HALF), :], w[0])
@@ -156,8 +158,15 @@
     halo_send(0, in_ref)
     for d in range(1, NZ):
         send(tab.at[0], tab.at[d], K_TAB + d - 1, at_z(d))
+    for buf in (xc3, xh3, d23, d13):
+        for h in range(5):
+            at = max(h * POS, 0)
+            buf[at:at + 32, :] = jnp.zeros((32, 3 * CH), BF)
+    acc[...] = jnp.zeros_like(acc)
+    loads[1].wait()
     turn(w2_ref, w2t, (0, 1, 2))
-    halo_recv(0)
+    loads[0].wait()
+    widen = halo_recv(0)
 
     def ag_key(right, s, j):
         return K_AG + (0 if right else 7) + (s * 2 + j if s < 3 else 6)
@@ -168,11 +177,12 @@
         send(src, dst, ag_key(right, s, j), at_z(1 if right else -1))
 
     for j in range(2):
+        lax.fori_loop(10 * j, 10 + 8 * j, widen, 0)
         pre = conv_map(tw_ref, j)
         feats[0, pl.ds(j * HALF, HALF), :] = (pre * jax.nn.sigmoid(pre)).astype(BF)
-        slope_map[pl.ds(j * HALF, HALF), :] = silu_slope(pre)
         ag_send(True, 0, j)
         ag_send(False, 0, j)
+        slope_map[pl.ds(j * HALF, HALF), :] = silu_slope(pre)
 
     for d in range(1, NZ):
         got(K_TAB + d - 1)
@@ -210,6 +220,9 @@
 
     take(0, 0)
     take(0, 1)
+
+    loads[2].wait()
+    loads[3].wait()
 
     def spread(i, carry):
         cotf[...] = cot_ref[i].astype(F32)
@@ -301,20 +314,17 @@
         for h in range(4):
             xt[:, h * POS:(h + 1) * POS] = buf[16 + h * POS:16 + (h + 1) * POS, CH:2 * CH].T
 
-        def one(a, carry):
-            at = pl.multiple_of(32 - a * 16, 16)
+        for a in range(3):
+            at = 32 - a * 16
             for b in range(3):
                 value = mm(xt[...], dbuf[pl.ds(at, 4 * POS), (2 - b) * CH:(3 - b) * CH])
                 low, high = value[:, 0:128], value[:, 128:256]
                 own[g, a * 3 + b] = jnp.where(core == 0, low, high)
                 snd[g, a * 3 + b] = jnp.where(core == 0, high, low).astype(BF)
-            return carry
-
-        lax.fori_loop(0, 3, one, 0)
-        for n in (2 * (1 - g), 2 * (1 - g) + 1):
-            t0, nt = PARTS[n][1:3]
-            span = pl.ds(t0, nt)
-            send(snd.at[g, span], rc.at[g, span], K_AR + n * AR_N, sibling)
+            if a > 0:
+                n = 2 * (1 - g) + a - 1
+                span = pl.ds(PARTS[n][1], PARTS[n][2])
+                send(snd.at[g, span], rc.at[g, span], K_AR + n * AR_N, sibling)
 
     def axes(n):
         if PARTS[n][3]:
@@ -360,6 +370,15 @@
             src = s2.at[n, pl.ds(0, nt), pl.ds(q * 16, 16), :]
             send(src, r2.at[n, d - 1, pl.ds(0, nt)], k + 3 + d, at2(d))
 
+    def owner(n, t):
+        return t + (0 if PARTS[n][1] == 0 else 4)
+
+    def z_copy(src, dst, ks, kr, to):
+        return pltpu.make_async_remote_copy(
+            src_ref=src, dst_ref=dst, send_sem=ssem.at[ks], recv_sem=rsem.at[kr],
+            device_id=(row, to), device_id_type=MESH,
+        )
+
     def ar3(n):
         nt = PARTS[n][2]
         k = K_AR + n * AR_N
@@ -370,53 +389,86 @@
         for d in range(3):
             v += r2[n, d, 0:nt].astype(F32)
         t3[n, 0:nt] = v
-        t3[n, nt:8] = jnp.zeros((8 - nt, 16, 128), F32)
         s3[n, 0:nt] = v.astype(BF)
-        s3[n, nt:8] = jnp.zeros((8 - nt, 16, 128), BF)
-        for d in range(1, NZ):
-            q = lax.rem(me + d, NZ)
-            send(s3.at[n, q], r3.at[n, d - 1], k + 6 + d, at_z(d))
+        for t in range(nt):
+            to = owner(n, t)
+
+            @pl.when(me != to)
+            def _():
+                z_copy(s3.at[n, t], r3.at[n, me], k + 7 + t, k + 7 + me, to).start()
 
     def ar4(n):
-        k = K_AR + n * AR_N
-        for d in range(1, NZ):
-            got(k + 6 + d)
-        v = t3[n, me]
-        for d in range(NZ - 1):
-            v += r3[n, d].astype(F32)
-        zb[n, me] = v.astype(BF)
-        for d in range(1, NZ):
-            send(zb.at[n, me], zb.at[n, me], k + 13 + d, at_z(d))
+        nt = PARTS[n][2]
+        k = K_AR + n * AR_N
+        first = owner(n, 0)
+
+        @pl.when((me >= first) & (me < first + nt))
+        def _():
+            for p in range(NZ):
+                @pl.when(me != p)
+                def _():
+                    z_copy(s3.at[n, 0], r3.at[n, p], k + 7, k + 7 + p, p).wait_recv()
+            v = t3[n, me - first]
+            for p in range(NZ):
+                v += jnp.where(me != p, r3[n, p].astype(F32), 0.0)
+            zb[n, me - first] = v.astype(BF)
+            part = zb.at[n, me - first]
+            for p in range(NZ):
+                @pl.when(me != p)
+                def _():
+                    z_copy(part, part, k + 15 + p, k + 15 + me - first, p).start()
 
     def ar5(n):
         g, t0, nt, _ = PARTS[n]
         k = K_AR + n * AR_N
         at1, p1, n1, at2, p2, n2 = axes(n)
-        for d in range(1, NZ):
-            got(k + 13 + d)
+        first = owner(n, 0)
+        for t in range(nt):
+            @pl.when(me != owner(n, t))
+            def _():
+                z_copy(zb.at[n, t], zb.at[n, t], k + 15, k + 15 + t, owner(n, t)).wait_recv()
         at = pl.multiple_of(p1 * 64 + p2 * 16, 16)
         gsum_ref[g, core, t0:t0 + nt, pl.ds(at, 16), :] = zb[n, 0:nt]
         part = gsum_ref.at[g, core, pl.ds(t0, nt), pl.ds(at, 16), :]
         for d in range(1, 4):
-            send(part, part, k + 20 + d, at2(d))
+            send(part, part, k + 22 + d, at2(d))
+
+    def z_sent(n):
+        nt = PARTS[n][2]
+        k = K_AR + n * AR_N
+        first = owner(n, 0)
+        for t in range(nt):
+            @pl.when(me != owner(n, t))
+            def _():
+                z_copy(s3.at[n, t], r3.at[n, me], k + 7 + t, k + 7, owner(n, t)).wait_send()
+
+        @pl.when((me >= first) & (me < first + nt))
+        def _():
+            for p in range(NZ):
+                @pl.when(me != p)
+                def _():
+                    z_copy(zb.at[n, 0], zb.at[n, 0], k + 15 + p, k + 15, p).wait_send()
 
     def ar6(n):
         g, t0, nt, _ = PARTS[n]
         k = K_AR + n * AR_N
         at1, p1, n1 = axes(n)[:3]
         for d in range(1, 4):
-            got(k + 20 + d)
+            got(k + 22 + d)
         part = gsum_ref.at[g, core, pl.ds(t0, nt), pl.ds(p1 * 64, 64), :]
         for d in range(1, 4):
-            send(part, part, k + 23 + d, at1(d))
+            send(part, part, k + 25 + d, at1(d))
+        send(part, part, k + 29, sibling)
 
     def ar7(n):
         g, t0, nt, _ = PARTS[n]
         k = K_AR + n * AR_N
-        for d in range(1, 4):
-            got(k + 23 + d)
-        part = gsum_ref.at[g, core, pl.ds(t0, nt)]
-        send(part, part, k + 27, sibling)
+        at1, p1, n1 = axes(n)[:3]
+        for d in (1, 3, 2):
+            got(k + 25 + d)
+            q = lax.rem(p1 - d + n1, n1)
+            part = gsum_ref.at[g, core, pl.ds(t0, nt), pl.ds(q * 64, 64), :]
+            send(part, part, k + 29 + d, sibling)
 
     def both(stage, g):
         stage(2 * (1 - g))
@@ -425,27 +477,31 @@
     wgrad(1, xh3, d23)
     for h in range(4):
         put(d13, h, cut(conv_box(d23, w2t, h) * slope1[h]))
+    wgrad(0, xc3, d13)
+    both(ar1, 1)
     for h in range(4):
         bg[h * POS:h * POS + 16, :] = jnp.zeros((16, CH), BF)
         bg[h * POS + 240:(h + 1) * POS, :] = jnp.zeros((16, CH), BF)
         bg[h * POS + 16:h * POS + 240, :] = conv_box(d13, w1t, h).astype(BF)
     rs_step(0)
-    both(ar1, 1)
     rs_step(1)
-    wgrad(0, xc3, d13)
+    both(ar1, 0)
+    both(ar2, 1)
     rs_step(2)
-    both(ar1, 0)
+    both(ar3, 1)
+    both(ar2, 0)
     rs_step(3)
-    both(ar2, 1)
+    both(ar3, 0)
     rs_step(4)
-    both(ar2, 0)
-    both(ar3, 1)
+    both(ar4, 1)
     rs_step(5)
-    both(ar3, 0)
-    both(ar4, 1)
-    rs_step(6)
     both(ar4, 0)
     both(ar5, 1)
+    rs_step(6)
+    both(ar5, 0)
+    both(ar6, 1)
+    both(ar6, 0)
+    both(ar7, 1)
 
     for j in range(2):
         total = term(0, j)
@@ -460,16 +516,14 @@
     scol[1, 0] = xf[:, 31, :].astype(BF)
     scol[1, 1] = xf[:, 0, :].astype(BF)
     halo_send(1, dm)
-    both(ar5, 0)
-    both(ar6, 1)
-    halo_recv(1)
+    both(ar7, 0)
+    lax.fori_loop(0, 18, halo_recv(1), 0)
     for j in range(2):
         gmap_ref[8 * j:8 * j + 8] = conv_map(twt, j).astype(BF).reshape(8, 32, CH)
-    both(ar6, 0)
-    both(ar7, 1)
-    both(ar7, 0)
     for n in range(4):
-        got(K_AR + n * AR_N + 27)
+        for d in range(4):
+            got(K_AR + n * AR_N + 29 + d)
+        z_sent(n)
     for k in sorted(live):
         live[k].wait_send()
 
@@ -485,6 +539,10 @@
 def step(in_map, tile_w, head_w1, head_w2, box_row, box_col, box_target, head_cot):
     vm = pltpu.VMEM
     scratch = [
+        vm((3, 3 * CH, CH), BF),
+        vm((3, 3 * CH, CH), BF),
+        vm((3, 3 * CH, CH), BF),
+        vm((14, 14, 4, CH), BF),
         vm((16, 32, CH), F32),
         vm((576, CH), BF),
         vm((576, 3 * CH), BF),
@@ -522,21 +580,23 @@
         vm((4, 5, 64, 128), F32),
         vm((4, 5, 64, 128), BF),
         vm((4, 3, 5, 16, 128), BF),
-        vm((4, NZ, 16, 128), F32),
+        vm((4, 5, 16, 128), F32),
+        vm((4, 5, 16, 128), BF),
         vm((4, NZ, 16, 128), BF),
-        vm((4, 7, 16, 128), BF),
-        vm((4, NZ, 16, 128), BF),
+        vm((4, 5, 16, 128), BF),
         pltpu.SemaphoreType.DMA((N_SEM,)),
         pltpu.SemaphoreType.DMA((N_SEM,)),
+        pltpu.SemaphoreType.DMA((4,)),
     ]
     in_vmem = pl.BlockSpec(memory_space=pltpu.VMEM)
+    in_any = pl.BlockSpec(memory_space=pl.ANY)
     grad_map, sums = pl.pallas_call(
         kernel,
         out_shape=(
             jax.ShapeDtypeStruct((16, 32, CH), BF),
             jax.ShapeDtypeStruct((2, 2, 9, 256, 128), BF),
         ),
-        in_specs=[in_vmem] * 8,
+        in_specs=[in_vmem] + [in_any] * 3 + [in_vmem] * 3 + [in_any],
         out_specs=(in_vmem, in_vmem),
         scratch_shapes=scratch,
         compiler_params=pltpu.CompilerParams(
@@ -555,7 +615,7 @@
     )
     grad_map, first, second = pl.pallas_call(
         finish,
-        grid=(3,),
+        grid=(1,),
         out_shape=(
             jax.ShapeDtypeStruct((16, 32, CH), BF),
             jax.ShapeDtypeStruct((9, CH, CH), F32),
@@ -563,12 +623,12 @@
         ),
         in_specs=[
             pl.BlockSpec((16, 32, CH), lambda i: (0, 0, 0)),
-            pl.BlockSpec((2, 2, 3, CH, 128), lambda i: (0, 0, i, 0, 0)),
+            pl.BlockSpec((2, 2, 9, CH, 128), lambda i: (0, 0, i, 0, 0)),
         ],
         out_specs=(
             pl.BlockSpec((16, 32, CH), lambda i: (0, 0, 0)),
-            pl.BlockSpec((3, CH, CH), lambda i: (i, 0, 0)),
-            pl.BlockSpec((3, CH, CH), lambda i: (i, 0, 0)),
+            pl.BlockSpec((9, CH, CH), lambda i: (i, 0, 0)),
+            pl.BlockSpec((9, CH, CH), lambda i: (i, 0, 0)),
         ),
     )(grad_map, sums)
     return grad_map, first.reshape(3, 3, CH, CH), second.reshape(3, 3, CH, CH)

time: 101 us -> 98.6 us (0.976)
  Pallas kernels: 101 us -> 97.8 us
    pallas_call x1, Pallas kernels: 96.2 us -> 93.5 us  [step(): pl.pallas_call(kernel, out_shape=(jax.ShapeDtypeStruct((16, 32, CH), BF),...]
where the time goes in v3:
time: 98.6 us; the launch traced here: 98.4 us
  Pallas kernels  97.8 us (99%)
    pallas_call x1, Pallas kernels, step(): pl.pallas_call(kernel, out_shape=(jax.ShapeDtypeStruct((16, 32, CH), BF),...  93.5 us
    pallas_call x1, Pallas kernels, step(): pl.pallas_call(finish, grid=(1,), out_shape=(jax.ShapeDtypeStruct((16, 32...  4.32 us

profile of v3, /device:TPU:1, one launch (start us, length us, event | category | flops | bytes accessed | tf_op | source)
XLA Modules:
  0.0 98.4 jit_solution(17995066413280342153)
XLA Ops:
  0.6 93.5 %shard_map.103 = (bf16[16,32,256]{2,1,0:T(8,128)(2,1)}, bf16[2,2,9,256,128]{4,3,2,1,0:T(8,128)(2,1)}) custom-call(bf16[16,32,256]{2,1,0:T(8,128)(2,1)} %in_ref.1, bf16[3,768,256]{2,1,0:T(8,128)(2,1)} %bitcast.13, bf16[3,768,256]{2,1,0:T(8,128)(2,1)} %bitcast.14, bf16[3,768,256]{2,1,0:T(8,128)(2,1)} %bitcast.15, s32[1,16]{1,0:T(1,128)} %bitcast.17, ...), custom_call_target="tpu_custom_call" | custom-call | flops 8000000000 | bytes 10000000 | tf_op jit(solution)/shard_map/pallas_call | solution.py:593
  94.1 4.3 %shard_map.104 = (bf16[16,32,256]{2,1,0:T(8,128)(2,1)}, f32[9,256,256]{2,1,0:T(8,128)}, f32[9,256,256]{2,1,0:T(8,128)}) custom-call(bf16[16,32,256]{2,1,0:T(8,128)(2,1)} %get-tuple-element.8.map_ref, bf16[2,2,9,256,128]{4,3,2,1,0:T(8,128)(2,1)} %get-tuple-element.9.sums_ref), custom_call_target="tpu_custom_call" | custom-call | tf_op jit(solution)/shard_map/pallas_call | solution.py:616

commit v4 on v3

--- a/solution.py
+++ b/solution.py
@@ -484,22 +484,22 @@
         bg[h * POS + 240:(h + 1) * POS, :] = jnp.zeros((16, CH), BF)
         bg[h * POS + 16:h * POS + 240, :] = conv_box(d13, w1t, h).astype(BF)
     rs_step(0)
+    both(ar1, 0)
     rs_step(1)
-    both(ar1, 0)
     both(ar2, 1)
     rs_step(2)
+    both(ar2, 0)
     both(ar3, 1)
-    both(ar2, 0)
+    both(ar3, 0)
     rs_step(3)
-    both(ar3, 0)
+    both(ar4, 1)
     rs_step(4)
-    both(ar4, 1)
-    rs_step(5)
     both(ar4, 0)
     both(ar5, 1)
-    rs_step(6)
+    rs_step(5)
     both(ar5, 0)
     both(ar6, 1)
+    rs_step(6)
     both(ar6, 0)
     both(ar7, 1)
 
@@ -528,12 +528,30 @@
         live[k].wait_send()
 
 
-def finish(map_ref, sums_ref, out_ref, first_ref, second_ref):
+def finish(map_ref, sums_ref, out_ref, first_ref, second_ref, held, made, isem, osem, msem):
     factor = 1.0 / math.sqrt(32 * 8 * 4 * 14 * 14)
-    out_ref[...] = map_ref[...]
-    for g, ref in enumerate((first_ref, second_ref)):
-        for half in range(2):
-            ref[:, :, half * 128:half * 128 + 128] = sums_ref[g, half].astype(F32) * factor
+    whole = pltpu.make_async_copy(map_ref, out_ref, msem)
+    whole.start()
+    loads, stores = [], []
+    for t in range(3):
+        span = pl.ds(3 * t, 3)
+        loads.append(pltpu.make_async_copy(sums_ref.at[:, :, span], held.at[:, :, span], isem.at[t]))
+        loads[t].start()
+    for t in range(3):
+        loads[t].wait()
+        for g, ref in enumerate((first_ref, second_ref)):
+            for half in range(2):
+                low = half * 128
+                made[g, 3 * t:3 * t + 3, :, low:low + 128] = (
+                    held[g, half, 3 * t:3 * t + 3].astype(F32) * factor
+                )
+            span = pl.ds(3 * t, 3)
+            store = pltpu.make_async_copy(made.at[g, span], ref.at[span], osem.at[2 * t + g])
+            store.start()
+            stores.append(store)
+    for store in stores:
+        store.wait()
+    whole.wait()
 
 
 def step(in_map, tile_w, head_w1, head_w2, box_row, box_col, box_target, head_cot):
@@ -615,21 +633,21 @@
     )
     grad_map, first, second = pl.pallas_call(
         finish,
-        grid=(1,),
         out_shape=(
             jax.ShapeDtypeStruct((16, 32, CH), BF),
             jax.ShapeDtypeStruct((9, CH, CH), F32),
             jax.ShapeDtypeStruct((9, CH, CH), F32),
         ),
-        in_specs=[
-            pl.BlockSpec((16, 32, CH), lambda i: (0, 0, 0)),
-            pl.BlockSpec((2, 2, 9, CH, 128), lambda i: (0, 0, i, 0, 0)),
+        in_specs=[in_any] * 2,
+        out_specs=(in_any,) * 3,
+        scratch_shapes=[
+            vm((2, 2, 9, CH, 128), BF),
+            vm((2, 9, CH, CH), F32),
+            pltpu.SemaphoreType.DMA((3,)),
+            pltpu.SemaphoreType.DMA((6,)),
+            pltpu.SemaphoreType.DMA,
         ],
-        out_specs=(
-            pl.BlockSpec((16, 32, CH), lambda i: (0, 0, 0)),
-            pl.BlockSpec((9, CH, CH), lambda i: (i, 0, 0)),
-            pl.BlockSpec((9, CH, CH), lambda i: (i, 0, 0)),
-        ),
+        compiler_params=pltpu.CompilerParams(vmem_limit_bytes=58 * 1024 * 1024),
     )(grad_map, sums)
     return grad_map, first.reshape(3, 3, CH, CH), second.reshape(3, 3, CH, CH)
 

time: 98.6 us -> 102 us (1.034)
  Pallas kernels: 97.8 us -> 101 us
    pallas_call x1, Pallas kernels: 4.32 us -> 9.13 us  [step(): pl.pallas_call(finish, out_shape=(jax.ShapeDtypeStruct((16, 32, CH), BF),...]
    pallas_call x1, Pallas kernels: 93.5 us -> 92.1 us  [step(): pl.pallas_call(kernel, out_shape=(jax.ShapeDtypeStruct((16, 32, CH), BF),...]
where the time goes in v4:
time: 102 us
  Pallas kernels  101 us (99%)
    pallas_call x1, Pallas kernels, step(): pl.pallas_call(kernel, out_shape=(jax.ShapeDtypeStruct((16, 32, CH), BF),...  92.1 us
    pallas_call x1, Pallas kernels, step(): pl.pallas_call(finish, out_shape=(jax.ShapeDtypeStruct((16, 32, CH), BF),...  9.13 us

profile of v4, /device:TPU:1, one launch (start us, length us, event | category | flops | bytes accessed | tf_op | source)
XLA Modules:
  0.0 102.0 jit_solution(5865961591699965674)
XLA Ops:
  0.6 92.1 %shard_map.103 = (bf16[16,32,256]{2,1,0:T(8,128)(2,1)}, bf16[2,2,9,256,128]{4,3,2,1,0:T(8,128)(2,1)}) custom-call(bf16[16,32,256]{2,1,0:T(8,128)(2,1)} %in_ref.1, bf16[3,768,256]{2,1,0:T(8,128)(2,1)} %bitcast.13, bf16[3,768,256]{2,1,0:T(8,128)(2,1)} %bitcast.14, bf16[3,768,256]{2,1,0:T(8,128)(2,1)} %bitcast.15, s32[1,16]{1,0:T(1,128)} %bitcast.17, ...), custom_call_target="tpu_custom_call" | custom-call | flops 8000000000 | bytes 10000000 | tf_op jit(solution)/shard_map/pallas_call | solution.py:611
  92.7 9.1 %shard_map.104 = (bf16[16,32,256]{2,1,0:T(8,128)(2,1)}, f32[9,256,256]{2,1,0:T(8,128)}, f32[9,256,256]{2,1,0:T(8,128)}) custom-call(bf16[16,32,256]{2,1,0:T(8,128)(2,1)} %get-tuple-element.8.map_ref, bf16[2,2,9,256,128]{4,3,2,1,0:T(8,128)(2,1)} %get-tuple-element.9.sums_ref), custom_call_target="tpu_custom_call" | custom-call | tf_op jit(solution)/shard_map/pallas_call | solution.py:634

commit v5 on v4

--- a/solution.py
+++ b/solution.py
@@ -528,10 +528,10 @@
         live[k].wait_send()
 
 
-def finish(map_ref, sums_ref, out_ref, first_ref, second_ref, held, made, isem, osem, msem):
+def finish(map_ref, sums_ref, out_ref, first_ref, second_ref, held, made, kept, isem, osem, msem):
     factor = 1.0 / math.sqrt(32 * 8 * 4 * 14 * 14)
-    whole = pltpu.make_async_copy(map_ref, out_ref, msem)
-    whole.start()
+    bring = pltpu.make_async_copy(map_ref, kept, msem.at[0])
+    bring.start()
     loads, stores = [], []
     for t in range(3):
         span = pl.ds(3 * t, 3)
@@ -549,9 +549,12 @@
             store = pltpu.make_async_copy(made.at[g, span], ref.at[span], osem.at[2 * t + g])
             store.start()
             stores.append(store)
+    bring.wait()
+    store = pltpu.make_async_copy(kept, out_ref, msem.at[1])
+    store.start()
+    stores.append(store)
     for store in stores:
         store.wait()
-    whole.wait()
 
 
 def step(in_map, tile_w, head_w1, head_w2, box_row, box_col, box_target, head_cot):
@@ -643,9 +646,10 @@
         scratch_shapes=[
             vm((2, 2, 9, CH, 128), BF),
             vm((2, 9, CH, CH), F32),
+            vm((16, 32, CH), BF),
             pltpu.SemaphoreType.DMA((3,)),
             pltpu.SemaphoreType.DMA((6,)),
-            pltpu.SemaphoreType.DMA,
+            pltpu.SemaphoreType.DMA((2,)),
         ],
         compiler_params=pltpu.CompilerParams(vmem_limit_bytes=58 * 1024 * 1024),
     )(grad_map, sums)

time: 102 us -> 96.6 us (0.947)
  Pallas kernels: 101 us -> 95.6 us
    pallas_call x1, Pallas kernels: 9.13 us -> 3.55 us  [step(): pl.pallas_call(finish, out_shape=(jax.ShapeDtypeStruct((16, 32, CH), BF),...]
where the time goes in v5:
time: 96.6 us; the launch traced here: 96.4 us
  Pallas kernels  95.6 us (99%)
    pallas_call x1, Pallas kernels, step(): pl.pallas_call(kernel, out_shape=(jax.ShapeDtypeStruct((16, 32, CH), BF),...  92.1 us
    pallas_call x1, Pallas kernels, step(): pl.pallas_call(finish, out_shape=(jax.ShapeDtypeStruct((16, 32, CH), BF),...  3.55 us

profile of v5, /device:TPU:1, one launch (start us, length us, event | category | flops | bytes accessed | tf_op | source)
XLA Modules:
  0.0 96.4 jit_solution(14476586210171220076)
XLA Ops:
  0.6 92.1 %shard_map.103 = (bf16[16,32,256]{2,1,0:T(8,128)(2,1)}, bf16[2,2,9,256,128]{4,3,2,1,0:T(8,128)(2,1)}) custom-call(bf16[16,32,256]{2,1,0:T(8,128)(2,1)} %in_ref.1, bf16[3,768,256]{2,1,0:T(8,128)(2,1)} %bitcast.13, bf16[3,768,256]{2,1,0:T(8,128)(2,1)} %bitcast.14, bf16[3,768,256]{2,1,0:T(8,128)(2,1)} %bitcast.15, s32[1,16]{1,0:T(1,128)} %bitcast.17, ...), custom_call_target="tpu_custom_call" | custom-call | flops 8000000000 | bytes 10000000 | tf_op jit(solution)/shard_map/pallas_call | solution.py:614
  92.7 3.5 %shard_map.104 = (bf16[16,32,256]{2,1,0:T(8,128)(2,1)}, f32[9,256,256]{2,1,0:T(8,128)}, f32[9,256,256]{2,1,0:T(8,128)}) custom-call(bf16[16,32,256]{2,1,0:T(8,128)(2,1)} %get-tuple-element.8.map_ref, bf16[2,2,9,256,128]{4,3,2,1,0:T(8,128)(2,1)} %get-tuple-element.9.sums_ref), custom_call_target="tpu_custom_call" | custom-call | tf_op jit(solution)/shard_map/pallas_call | solution.py:637

commit v6 on v5

--- a/solution.py
+++ b/solution.py
@@ -300,10 +300,12 @@
         return K_RS + (0 if right else 7) + k
 
     def rs_step(k):
+        work = []
         for right in (True, False):
             d, j = rs_item(right, k)
+            work.append((right, term(d if right else -d, j)))
+        for right, value in work:
             side = 0 if right else 1
-            value = term(d if right else -d, j)
             if k >= 2:
                 got(rs_key(right, k - 2))
                 value += rs_r[side, k - 2].astype(F32)

time: 96.6 us -> 96.2 us (level)
  no operation moved by 1% of the time
where the time goes in v6:
time: 96.2 us; the launch traced here: 96.1 us
  Pallas kernels  95.3 us (99%)
    pallas_call x1, Pallas kernels, step(): pl.pallas_call(kernel, out_shape=(jax.ShapeDtypeStruct((16, 32, CH), BF),...  91.7 us
    pallas_call x1, Pallas kernels, step(): pl.pallas_call(finish, out_shape=(jax.ShapeDtypeStruct((16, 32, CH), BF),...  3.55 us

profile of v6, /device:TPU:1, one launch (start us, length us, event | category | flops | bytes accessed | tf_op | source)
XLA Modules:
  0.0 96.1 jit_solution(12663319123690734170)
XLA Ops:
  0.6 91.7 %shard_map.103 = (bf16[16,32,256]{2,1,0:T(8,128)(2,1)}, bf16[2,2,9,256,128]{4,3,2,1,0:T(8,128)(2,1)}) custom-call(bf16[16,32,256]{2,1,0:T(8,128)(2,1)} %in_ref.1, bf16[3,768,256]{2,1,0:T(8,128)(2,1)} %bitcast.13, bf16[3,768,256]{2,1,0:T(8,128)(2,1)} %bitcast.14, bf16[3,768,256]{2,1,0:T(8,128)(2,1)} %bitcast.15, s32[1,16]{1,0:T(1,128)} %bitcast.17, ...), custom_call_target="tpu_custom_call" | custom-call | flops 8000000000 | bytes 10000000 | tf_op jit(solution)/shard_map/pallas_call | solution.py:616
  92.4 3.5 %shard_map.104 = (bf16[16,32,256]{2,1,0:T(8,128)(2,1)}, f32[9,256,256]{2,1,0:T(8,128)}, f32[9,256,256]{2,1,0:T(8,128)}) custom-call(bf16[16,32,256]{2,1,0:T(8,128)(2,1)} %get-tuple-element.8.map_ref, bf16[2,2,9,256,128]{4,3,2,1,0:T(8,128)(2,1)} %get-tuple-element.9.sums_ref), custom_call_target="tpu_custom_call" | custom-call | tf_op jit(solution)/shard_map/pallas_call | solution.py:639
